TPU v7x, 128 devices: a whole 4x4x4 slice. The times are simulated.
128 devices in a mesh: fsdp: 32 (over y, z, core), ctx: 2 (over x_lo), tp: 2 (over x_hi).
Axes of the slice: x: 4 (x_hi: 2, x_lo: 2; x = x_hi * 2 + x_lo), y: 4, z: 4, core: 2. Of those that a mesh axis runs over, the one named last changes fastest.
Arguments:
- tokens: bfloat16 [32, 1024, 1024], P('fsdp', 'ctx'), may hold values from -6 to 6
- segments: int32 [32, 1024], P('fsdp'), may hold values from 0 to 3, as said below
- cotangent: bfloat16 [32, 1024, 1024], P('fsdp', 'ctx'), may hold values from -6 to 6
- gain_mixer: bfloat16 [1024], P('fsdp'), may hold values from 0.5 to 1.5
- gain_ffn: bfloat16 [1024], P('fsdp'), may hold values from 0.5 to 1.5
- query_proj: bfloat16 [1024, 512], P('fsdp', 'tp'), may hold values from -0.1875 to 0.1875
- key_value_weight: bfloat16 [1024, 2, 128], P('fsdp', None, 'tp'), may hold values from -0.1875 to 0.1875
- attn_out: bfloat16 [512, 1024], P('tp', 'fsdp'), may hold values from -2 to 2
- inner_proj: bfloat16 [1024, 2, 1536], P('fsdp', None, 'tp'), may hold values from -0.1875 to 0.1875
- state_proj: bfloat16 [1024, 256], P('fsdp'), may hold values from -0.1875 to 0.1875
- step_proj: bfloat16 [1024, 24], P('fsdp', 'tp'), may hold values from -0.09375 to 0.09375
- conv_inner: bfloat16 [4, 1536], P(None, 'tp'), may hold values from -3 to 3
- conv_state: bfloat16 [4, 256], replicated, may hold values from -3 to 3
- decay_log: float32 [24], P('tp'), may hold values from 0 to 2.77
- step_bias: float32 [24], P('tp'), may hold values from -6.9 to -2.3
- skip_gain: float32 [24], P('tp'), may hold values from 0.5 to 2
- inner_out: bfloat16 [1536, 1024], P('tp', 'fsdp'), may hold values from -0.15625 to 0.15625
- gate_up: bfloat16 [1024, 2, 2048], P('fsdp', None, 'tp'), may hold values from -0.1875 to 0.1875
- down_proj: bfloat16 [2048, 1024], P('tp', 'fsdp'), may hold values from -0.125 to 0.125
Outputs:
- block_out: bfloat16 [32, 1024, 1024], P('fsdp', 'ctx')
- tokens_grad: float32 [32, 1024, 1024], P('fsdp', 'ctx')
- gain_mixer_grad: float32 [1024], P('fsdp')
- gain_ffn_grad: float32 [1024], P('fsdp')
- query_proj_grad: float32 [1024, 512], P('fsdp', 'tp')
- keyval_proj_grad: float32 [1024, 2, 128], P('fsdp', None, 'tp')
- attn_out_grad: float32 [512, 1024], P('tp', 'fsdp')
- inner_proj_grad: float32 [1024, 2, 1536], P('fsdp', None, 'tp')
- state_proj_grad: float32 [1024, 256], P('fsdp')
- step_proj_grad: float32 [1024, 24], P('fsdp', 'tp')
- conv_inner_grad: float32 [4, 1536], P(None, 'tp')
- conv_state_grad: float32 [4, 256], replicated
- decay_log_grad: float32 [24], P('tp')
- step_bias_grad: float32 [24], P('tp')
- skip_gain_grad: float32 [24], P('tp')
- inner_out_grad: float32 [1536, 1024], P('tp', 'fsdp')
- gate_up_grad: float32 [1024, 2, 2048], P('fsdp', None, 'tp')
- down_proj_grad: float32 [2048, 1024], P('tp', 'fsdp')
Inputs may be any that keep to these rules, and one draw needn't show every extreme that they name: `segments`: segment numbers of a sequence start at 0, never fall and rise by at most one from a token to the next; every sequence holds four documents, and each document has at least 60 tokens.
All inputs are finite; a program needn't handle non-finite values.
Results may differ from a plain program's by a relative error of at most 0.029.
Values may be sent and summed in bfloat16 or wider, within the bound.
A program may use at most 192 MiB of HBM per device.

v0:
```python
import math

import jax
import jax.numpy as jnp
from jax import lax
from jax.sharding import PartitionSpec as P

HEAD_WIDTH = 64


eps_norm = 1e-05
neg_large = -1e30
rope_base = 100000000000.0
highest = lax.Precision.HIGHEST


def sent_to_all(array, axis):
    devices = lax.axis_size(axis)
    return lax.all_to_all(
        jnp.broadcast_to(array[None], (devices, *array.shape)), axis, 0, 0, tiled=True
    )


def over_copies(array, axis):
    return sent_to_all(array, axis).sum(axis=0)


def turned_gather(arrays, axis, dims):
    turned = [jnp.moveaxis(a, dim, 0) for a, dim in zip(arrays, dims)]
    both = jnp.concatenate([t.reshape(len(t), -1) for t in turned], axis=1)
    result, at, finished = (lax.all_gather(both, axis, axis=0, tiled=True), 0, [])
    for t, dim in zip(turned, dims):
        section = result[:, at : at + t[0].size].reshape(-1, *t.shape[1:])
        finished.append(jnp.moveaxis(section, 0, dim))
        at += t[0].size
    return tuple(finished)


def passed_along(block, axis, distance):
    devices = range(lax.axis_size(axis))
    route = [(i - distance, i) for i in devices if i - distance in devices]
    return lax.ppermute(block, axis, route)


def combined_pairwise(pieces, combine):
    while len(jax.tree.leaves(pieces)[0]) > 1:
        pieces = jax.vmap(combine)(
            *(jax.tree.map(lambda part: part[side::2], pieces) for side in (0, 1))
        )
    return jax.tree.map(lambda part: part[0], pieces)


def prefix(array, axis, combine, identity):
    devices, place = (lax.axis_size(axis), lax.axis_index(axis))
    passed = jnp.arange(devices) < place

    def prefix_kept(part, zero, own):
        part = jnp.where(
            passed.reshape(-1, *(1 for _ in own.shape)),
            part.astype(own.dtype),
            jnp.asarray(zero, own.dtype),
        )
        return part

    pieces = jax.tree.map(
        lambda part: sent_to_all(part, axis),
        jax.tree.map(lambda part, kind: part.astype(kind), array, (jnp.bfloat16, jnp.bfloat16)),
    )
    return combined_pairwise(jax.tree.map(prefix_kept, pieces, identity, array), combine)


def entering_2(array, axis, combine, identity):
    devices, place = (lax.axis_size(axis), lax.axis_index(axis))
    passed = jnp.arange(devices) > place

    def entering_kept(part, zero, own):
        part = jnp.where(
            passed.reshape(-1, *(1 for _ in own.shape)),
            part.astype(own.dtype),
            jnp.asarray(zero, own.dtype),
        )
        return part[::-1]

    pieces = jax.tree.map(
        lambda part: sent_to_all(part, axis),
        jax.tree.map(
            lambda part, kind: part.astype(kind),
            array,
            jax.tree.map(lambda a: jnp.bfloat16 if a.dtype == jnp.float32 else a.dtype, array),
        ),
    )
    return combined_pairwise(jax.tree.map(entering_kept, pieces, identity, array), combine)


def sent_together(arrays, axis, dim, along):
    columns = [a.reshape(*a.shape[:along], -1) for a in arrays]
    both = jnp.concatenate(columns, axis=along)
    result, at, finished = (lax.psum_scatter(both, axis, scatter_dimension=dim, tiled=True), 0, [])
    for a, column in zip(arrays, columns):
        section = result[..., at : at + column.shape[along]]
        finished.append(section.reshape(*section.shape[:along], *a.shape[along:]))
        at += column.shape[along]
    return tuple(finished)


def taken_together(array, axis):
    everything = sent_to_all(array, axis)
    return jnp.sum(everything.astype(jnp.float32), axis=0)


def together(arrays, axis):
    vector, at, finished = (jnp.concatenate([a.reshape(-1) for a in arrays]), 0, [])
    total = over_copies(vector, axis)
    for a in arrays:
        finished.append(total[at : at + a.size].reshape(a.shape))
        at += a.size
    return tuple(finished)


def rms_norm(values, gain_vec):
    return (
        values * lax.rsqrt(jnp.mean(values * values, axis=-1, keepdims=True) + eps_norm) * gain_vec
    )


def rope_tables(positions, rot_width):
    indices = jnp.arange(rot_width // 2).astype(jnp.float32)
    frequency = jnp.exp(indices * (-2.0 * math.log(rope_base) / rot_width))
    angles = positions[:, None] * frequency[None, :]
    return (jnp.cos(angles), jnp.sin(angles))


def rotary_rotate(vectors, cosine_table, sine_table):
    halfway = vectors.shape[-1] // 2
    front_half = vectors[..., :halfway]
    back_part = vectors[..., halfway:]
    cos_b = cosine_table[:, None, :]
    sin_b = sine_table[:, None, :]
    return jnp.concatenate(
        [front_half * cos_b - back_part * sin_b, back_part * cos_b + front_half * sin_b], axis=-1
    )


def conv_silu(current, rim_rows, weight, seg_now, seg_rim):
    conv_taps = weight.shape[0]
    span_rows = current.shape[0]
    extended = jnp.concatenate([rim_rows, current], axis=0)
    seg_ext = jnp.concatenate([seg_rim, seg_now], axis=0)
    running = jnp.zeros_like(current)
    for offset in range(conv_taps):
        window = lax.slice_in_dim(extended, offset, offset + span_rows, axis=0)
        same_doc = (
            lax.slice_in_dim(seg_ext, offset, offset + span_rows, axis=0) == seg_now
        ).astype(jnp.float32)
        running = running + window * weight[offset][None, :] * same_doc[:, None]
    return jax.nn.silu(running)


def span_step(carry, pieces):
    state_now, seg_last = carry
    x_scaled, b_mat, c_mat, log_decay, seg_now = pieces
    span_rows = seg_now.shape[0]
    lower_tri = jnp.arange(span_rows)[:, None] >= jnp.arange(span_rows)[None, :]
    cumulative = jnp.cumsum(log_decay, axis=0)
    same_doc = lower_tri & (seg_now[:, None] == seg_now[None, :])
    decays = jnp.exp(
        jnp.where(same_doc[:, :, None], cumulative[:, None, :] - cumulative[None, :, :], neg_large)
    )
    intersection = jnp.dot(c_mat, b_mat.T, precision=highest, preferred_element_type=jnp.float32)
    intra_out = jnp.einsum(
        "tsh,shp->thp", decays * intersection[:, :, None], x_scaled, precision=highest
    )
    carry_on = (seg_now == seg_last).astype(jnp.float32)
    entering = jnp.exp(cumulative) * carry_on[:, None]
    from_state = (
        jnp.einsum("tn,hpn->thp", c_mat, state_now, precision=highest) * entering[:, :, None]
    )
    last_seg = seg_now[span_rows - 1]
    tail_decay = jnp.exp(
        jnp.where(
            (seg_now == last_seg)[:, None],
            cumulative[span_rows - 1][None, :] - cumulative,
            neg_large,
        )
    )
    new_state = state_now * entering[span_rows - 1][:, None, None] + jnp.einsum(
        "shp,sn->hpn", x_scaled * tail_decay[:, :, None], b_mat, precision=highest
    )
    return ((new_state, last_seg), intra_out + from_state)


def ssd_scan(x_scaled, b_mat, c_mat, log_decay, seg_now, seg_before, state_start):
    total_rows = seg_now.shape[0]
    span_len = math.gcd(128, total_rows)
    pieces = tuple(
        (
            array.reshape((total_rows // span_len, span_len) + array.shape[1:])
            for array in (x_scaled, b_mat, c_mat, log_decay, seg_now)
        )
    )
    (final_state, last_seg), span_outs = lax.scan(
        jax.checkpoint(span_step), (state_start, seg_before), pieces
    )
    return (span_outs.reshape(x_scaled.shape), final_state)


def block_state(x_scaled, b_mat, log_decay, seg_now, seg_before):
    cumulative = jnp.cumsum(log_decay, axis=0)
    last_seg = seg_now[-1]
    tail_decay = jnp.exp(
        jnp.where((seg_now == last_seg)[:, None], cumulative[-1][None, :] - cumulative, neg_large)
    )
    state_end = jnp.einsum(
        "shp,sn->hpn", x_scaled * tail_decay[:, :, None], b_mat, precision=highest
    )
    carry_on = (last_seg == seg_before).astype(jnp.float32)
    return (state_end, jnp.exp(cumulative[-1]) * carry_on)


def ssd_pull(x_scaled, b_mat, c_mat, log_decay, seg_now, seg_before, state_start, grad_out):

    def forward(scaled_in, b_input, c_input, decay_in, start_in):
        return ssd_scan(scaled_in, b_input, c_input, decay_in, seg_now, seg_before, start_in)[0]

    _unused, pullback = jax.vjp(forward, x_scaled, b_mat, c_mat, log_decay, state_start)
    return pullback(grad_out)


def state_pull(x_scaled, b_mat, log_decay, seg_now, seg_before, grad_state, grad_gain):

    def forward(scaled_in, b_input, decay_in):
        return block_state(scaled_in, b_input, decay_in, seg_now, seg_before)

    _unused, pullback = jax.vjp(forward, x_scaled, b_mat, log_decay)
    return pullback((grad_state, grad_gain))


def chain_combine(earlier, later):
    return (later[1][..., None, None] * earlier[0] + later[0], earlier[1] * later[1])


def per_sequence(step_fn, arrays):
    return lax.map(lambda items: step_fn(*items), arrays)


def head_total(partial_sum):
    return over_copies(partial_sum, "tp")


def shards(
    tokens,
    segments,
    cotangent,
    gain_mixer,
    gain_ffn,
    query_proj,
    key_value_weight,
    attn_out,
    inner_proj,
    state_proj,
    step_proj,
    conv_inner,
    conv_state,
    decay_log,
    step_bias,
    skip_gain,
    inner_out,
    gate_up,
    down_proj,
):
    f32 = jnp.float32
    bf16 = jnp.bfloat16
    seq_count, tok_rows, width_all = tokens.shape
    flat_rows = seq_count * tok_rows
    gathered = turned_gather(
        (
            gain_mixer,
            gain_ffn,
            query_proj,
            key_value_weight,
            attn_out,
            inner_proj,
            state_proj,
            step_proj,
            inner_out,
            gate_up,
            down_proj,
        ),
        "fsdp",
        (0, 0, 0, 0, 1, 0, 0, 0, 1, 0, 1),
    )
    (
        gain_in_w,
        gain_ff_w,
        wq_all,
        wkv_all,
        wo_all,
        wzx_all,
        wbc_all,
        wdt_all,
        wout_all,
        wgu_all,
        wdown_all,
    ) = gathered
    gain_in32 = gain_in_w.astype(f32)
    gain_ff32 = gain_ff_w.astype(f32)
    wkv_flat = wkv_all.reshape(width_all, -1)
    wzx_flat = wzx_all.reshape(width_all, -1)
    wgu_flat = wgu_all.reshape(width_all, -1)
    key_width = wkv_flat.shape[1] // 2
    inner_width = wzx_flat.shape[1] // 2
    hidden_half = wgu_flat.shape[1] // 2
    scan_heads = decay_log.shape[0]
    head_size = inner_width // scan_heads
    state_size = wbc_all.shape[1] // 2
    query_heads = wq_all.shape[1] // HEAD_WIDTH
    keyval_heads = key_width // HEAD_WIDTH
    query_group_width = query_heads // keyval_heads
    score_scale = HEAD_WIDTH ** (-0.5)
    conv_taps = conv_inner.shape[0]
    ctx_index = lax.axis_index("ctx")
    row_start = ctx_index * tok_rows
    seg_now = lax.dynamic_slice_in_dim(segments, row_start, tok_rows, 1)
    earlier_seg = lax.dynamic_slice_in_dim(
        segments, jnp.maximum(row_start - tok_rows, 0), tok_rows, 1
    )
    seg_prior = jnp.where(ctx_index > 0, earlier_seg, -1)
    seg_before = seg_prior[:, tok_rows - 1]
    seg_rim = seg_prior[:, tok_rows - (conv_taps - 1) :]

    def attention_mask(seg_row, prior_row):
        query_pos = row_start + jnp.arange(tok_rows)
        key_pos = row_start - tok_rows + jnp.arange(2 * tok_rows)
        key_seg = jnp.concatenate([prior_row, seg_row])
        return (key_pos[None, :] <= query_pos[:, None]) & (key_seg[None, :] == seg_row[:, None])

    def split_pack(own_pack, prior_pack):
        packed = jnp.concatenate([prior_pack, own_pack], axis=0)
        every_key = packed[:, :key_width].reshape(2 * tok_rows, keyval_heads, HEAD_WIDTH)
        every_value = packed[:, key_width:].reshape(2 * tok_rows, keyval_heads, HEAD_WIDTH)
        return (every_key, every_value)

    def score_rows(query_rows, every_key, key_mask):
        grouped_heads = query_rows.reshape(tok_rows, keyval_heads, query_group_width, HEAD_WIDTH)
        scores = (
            jnp.einsum("qkgd,tkd->kgqt", grouped_heads, every_key, preferred_element_type=f32)
            * score_scale
        )
        return (grouped_heads, jnp.where(key_mask[None, None], scores, neg_large))

    def attend_forward(query_rows, own_pack, prior_pack, seg_row, prior_row):
        every_key, every_value = split_pack(own_pack, prior_pack)
        grouped_heads, scores = score_rows(
            query_rows, every_key, attention_mask(seg_row, prior_row)
        )
        row_max = jnp.max(scores, axis=-1, keepdims=True)
        shifted = jnp.exp(scores - row_max)
        totals = jnp.sum(shifted, axis=-1, keepdims=True)
        weights_b = (shifted / totals).astype(bf16)
        mixed = jnp.einsum("kgqt,tkd->qkgd", weights_b, every_value, preferred_element_type=f32)
        return (mixed.reshape(tok_rows, -1).astype(bf16), row_max + jnp.log(totals))

    def attend_backward(
        query_rows, own_pack, prior_pack, seg_row, prior_row, log_totals, grad_rows
    ):
        every_key, every_value = split_pack(own_pack, prior_pack)
        grouped_heads, scores = score_rows(
            query_rows, every_key, attention_mask(seg_row, prior_row)
        )
        weights = jnp.exp(scores - log_totals)
        weights_b = weights.astype(bf16)
        grad_heads = grad_rows.reshape(tok_rows, keyval_heads, query_group_width, HEAD_WIDTH)
        grad_values = jnp.einsum(
            "kgqt,qkgd->tkd", weights_b, grad_heads, preferred_element_type=f32
        )
        grad_weights = jnp.einsum(
            "qkgd,tkd->kgqt", grad_heads, every_value, preferred_element_type=f32
        )
        grad_scores = (
            weights * (grad_weights - jnp.sum(weights * grad_weights, axis=-1, keepdims=True))
        ).astype(bf16)
        grad_query = (
            jnp.einsum("kgqt,tkd->qkgd", grad_scores, every_key, preferred_element_type=f32)
            * score_scale
        )
        grad_keys = (
            jnp.einsum("kgqt,qkgd->tkd", grad_scores, grouped_heads, preferred_element_type=f32)
            * score_scale
        )
        grad_pack = jnp.concatenate(
            [
                grad_keys.reshape(2 * tok_rows, key_width),
                grad_values.reshape(2 * tok_rows, key_width),
            ],
            axis=1,
        )
        return (grad_query.reshape(tok_rows, -1), grad_pack)

    residual = tokens.astype(f32).reshape(flat_rows, width_all)
    normalized_input = rms_norm(residual, gain_in32)
    normed_b = normalized_input.astype(bf16)
    query_lin = jnp.dot(normed_b, wq_all, preferred_element_type=f32)
    key_value_linear = jnp.dot(normed_b, wkv_flat, preferred_element_type=f32)
    inner_lin = jnp.dot(normed_b, wzx_flat, preferred_element_type=f32)
    state_lin = jnp.dot(normed_b, wbc_all, preferred_element_type=f32)
    step_lin = jnp.dot(normed_b, wdt_all, preferred_element_type=f32)
    positions = (row_start + jnp.arange(tok_rows)).astype(f32)
    cosine_table, sine_table = rope_tables(positions, HEAD_WIDTH)
    queries_b = rotary_rotate(
        query_lin.reshape(seq_count, tok_rows, query_heads, HEAD_WIDTH), cosine_table, sine_table
    ).astype(bf16)
    keys_b = rotary_rotate(
        key_value_linear[:, :key_width].reshape(seq_count, tok_rows, keyval_heads, HEAD_WIDTH),
        cosine_table,
        sine_table,
    ).astype(bf16)
    values_b = key_value_linear[:, key_width:].astype(bf16).reshape(seq_count, tok_rows, key_width)
    key_pack = jnp.concatenate([keys_b.reshape(seq_count, tok_rows, key_width), values_b], axis=-1)
    prior_pack = passed_along(key_pack, "ctx", 1)
    attended_b, lse_kept = per_sequence(
        attend_forward, (queries_b, key_pack, prior_pack, seg_now, seg_prior)
    )
    gate_z = inner_lin[:, :inner_width]
    conv_in = jnp.concatenate([inner_lin[:, inner_width:], state_lin], axis=1).reshape(
        seq_count, tok_rows, -1
    )
    rim_in = passed_along(conv_in[:, tok_rows - (conv_taps - 1) :], "ctx", 1)
    conv_weight = jnp.concatenate([conv_inner, conv_state], axis=1).astype(f32)

    def conv_forward(current, rim_rows, seg_row, rim_seg):
        return conv_silu(current, rim_rows, conv_weight, seg_row, rim_seg)

    conv_out = per_sequence(conv_forward, (conv_in, rim_in, seg_now, seg_rim))
    x_heads = conv_out[..., :inner_width].reshape(seq_count, tok_rows, scan_heads, head_size)
    b_mat = conv_out[..., inner_width : inner_width + state_size]
    c_mat = conv_out[..., inner_width + state_size :]
    step_pre = step_lin.reshape(seq_count, tok_rows, scan_heads) + step_bias
    step_size = jax.nn.softplus(step_pre)
    decay_rate = -jnp.exp(decay_log)
    log_decay = step_size * decay_rate
    x_scaled = x_heads * step_size[..., None]
    local_state, local_gain = per_sequence(
        block_state, (x_scaled, b_mat, log_decay, seg_now, seg_before)
    )
    incoming, carried_gain = prefix(
        (local_state, local_gain),
        "ctx",
        chain_combine,
        (jnp.zeros_like(local_state), jnp.ones_like(local_gain)),
    )

    def ssd_forward(scaled_in, b_input, c_input, decay_in, seg_row, before_seg, start_in):
        return ssd_scan(scaled_in, b_input, c_input, decay_in, seg_row, before_seg, start_in)[0]

    ssd_out = per_sequence(
        ssd_forward, (x_scaled, b_mat, c_mat, log_decay, seg_now, seg_before, incoming)
    )
    y_flat = (ssd_out + x_heads * skip_gain[:, None]).reshape(flat_rows, inner_width)
    silu_z = jax.nn.silu(gate_z)
    gated_b = (y_flat * silu_z).astype(bf16)
    attn_flat = attended_b.reshape(flat_rows, -1)
    branch_part = jnp.dot(attn_flat, wo_all, preferred_element_type=f32) + jnp.dot(
        gated_b, wout_all, preferred_element_type=f32
    )
    mid_stream = residual + head_total(branch_part)
    normed_ff = rms_norm(mid_stream, gain_ff32)
    normed_ff_b = normed_ff.astype(bf16)
    gu_lin = jnp.dot(normed_ff_b, wgu_flat, preferred_element_type=f32)
    gate_lin = gu_lin[:, :hidden_half]
    up_lin = gu_lin[:, hidden_half:]
    sig_gate = jax.nn.sigmoid(gate_lin)
    silu_gate = gate_lin * sig_gate
    act_b = (silu_gate * up_lin).astype(bf16)
    ffn_sum = head_total(jnp.dot(act_b, wdown_all, preferred_element_type=f32))
    result = (mid_stream + ffn_sum).astype(bf16).reshape(seq_count, tok_rows, width_all)
    cot_b = cotangent.reshape(flat_rows, width_all)
    grad_down = jnp.dot(act_b.T, cot_b, preferred_element_type=f32)
    grad_act = jnp.dot(cot_b, wdown_all.T, preferred_element_type=f32)
    grad_gate = grad_act * up_lin * sig_gate * (1.0 + gate_lin * (1.0 - sig_gate))
    grad_up = grad_act * silu_gate
    grad_gu_b = jnp.concatenate([grad_gate, grad_up], axis=1).astype(bf16)
    grad_gu_w = jnp.dot(normed_ff_b.T, grad_gu_b, preferred_element_type=f32).reshape(wgu_all.shape)
    grad_normed_ff = head_total(jnp.dot(grad_gu_b, wgu_flat.T, preferred_element_type=f32))
    _unused, norm_pull = jax.vjp(rms_norm, mid_stream, gain_ff32)
    grad_mid_norm, grad_gain_ff = norm_pull(grad_normed_ff)
    grad_mid = cotangent.astype(f32).reshape(flat_rows, width_all) + grad_mid_norm
    grad_mid_b = grad_mid.astype(bf16)
    grad_o_w = jnp.dot(attn_flat.T, grad_mid_b, preferred_element_type=f32)
    grad_attn_b = jnp.dot(grad_mid_b, wo_all.T, preferred_element_type=f32).astype(bf16)
    grad_out_w = jnp.dot(gated_b.T, grad_mid_b, preferred_element_type=f32)
    grad_gated = jnp.dot(grad_mid_b, wout_all.T, preferred_element_type=f32)
    grad_y = grad_gated * silu_z
    sig_z = jax.nn.sigmoid(gate_z)
    grad_z = grad_gated * y_flat * sig_z * (1.0 + gate_z * (1.0 - sig_z))
    grad_y_heads = grad_y.reshape(seq_count, tok_rows, scan_heads, head_size)
    grad_skip = jnp.sum(grad_y_heads * x_heads, axis=(0, 1, 3))
    grad_xs_two, grad_b_two, grad_c_two, grad_ld_two, grad_incoming = per_sequence(
        ssd_pull, (x_scaled, b_mat, c_mat, log_decay, seg_now, seg_before, incoming, grad_y_heads)
    )
    later_grad, later_gain = entering_2(
        (grad_incoming, local_gain),
        "ctx",
        chain_combine,
        (jnp.zeros_like(grad_incoming), jnp.ones_like(local_gain)),
    )
    grad_gain_local = jnp.sum(later_grad * incoming, axis=(2, 3))
    grad_xs_one, grad_b_one, grad_ld_one = per_sequence(
        state_pull, (x_scaled, b_mat, log_decay, seg_now, seg_before, later_grad, grad_gain_local)
    )
    grad_scaled = grad_xs_one + grad_xs_two
    grad_log = grad_ld_one + grad_ld_two
    grad_x_heads = grad_y_heads * skip_gain[:, None] + grad_scaled * step_size[..., None]
    grad_step = jnp.sum(grad_scaled * x_heads, axis=-1) + grad_log * decay_rate
    grad_decay_log = jnp.sum(grad_log * step_size, axis=(0, 1)) * decay_rate
    grad_step_pre = grad_step * jax.nn.sigmoid(step_pre)
    grad_step_bias = jnp.sum(grad_step_pre, axis=(0, 1))
    grad_step_b = grad_step_pre.reshape(flat_rows, scan_heads).astype(bf16)
    grad_bc_post = head_total(jnp.concatenate([grad_b_one + grad_b_two, grad_c_two], axis=-1))
    grad_conv_out = jnp.concatenate(
        [grad_x_heads.reshape(seq_count, tok_rows, inner_width), grad_bc_post], axis=-1
    )

    def conv_pull(current, rim_rows, seg_row, rim_seg, grad_rows):

        def forward(current_in, rim_input, weight_in):
            return conv_silu(current_in, rim_input, weight_in, seg_row, rim_seg)

        _unused_out, pullback = jax.vjp(forward, current, rim_rows, conv_weight)
        return pullback(grad_rows)

    grad_conv_in, grad_rim, grad_taps = per_sequence(
        conv_pull, (conv_in, rim_in, seg_now, seg_rim, grad_conv_out)
    )
    rim_back = passed_along(grad_rim, "ctx", -1)
    grad_conv_in = jnp.concatenate(
        [
            grad_conv_in[:, : tok_rows - (conv_taps - 1)],
            grad_conv_in[:, tok_rows - (conv_taps - 1) :] + rim_back,
        ],
        axis=1,
    )
    grad_taps = jnp.sum(grad_taps, axis=0)
    grad_conv_flat = grad_conv_in.reshape(flat_rows, -1)
    grad_zx_b = jnp.concatenate([grad_z, grad_conv_flat[:, :inner_width]], axis=1).astype(bf16)
    grad_bc_b = grad_conv_flat[:, inner_width:].astype(bf16)
    grad_query, grad_pack = per_sequence(
        attend_backward,
        (
            queries_b,
            key_pack,
            prior_pack,
            seg_now,
            seg_prior,
            lse_kept,
            grad_attn_b.reshape(seq_count, tok_rows, -1),
        ),
    )
    pack_back = passed_along(grad_pack[:, :tok_rows].astype(jnp.bfloat16), "ctx", -1).astype(
        jnp.float32
    )
    grad_own_pack = grad_pack[:, tok_rows:] + pack_back
    grad_keys = rotary_rotate(
        grad_own_pack[..., :key_width].reshape(seq_count, tok_rows, keyval_heads, HEAD_WIDTH),
        cosine_table,
        -sine_table,
    )
    grad_kv_b = jnp.concatenate(
        [
            grad_keys.reshape(flat_rows, key_width),
            grad_own_pack[..., key_width:].reshape(flat_rows, key_width),
        ],
        axis=1,
    ).astype(bf16)
    grad_q_b = (
        rotary_rotate(
            grad_query.reshape(seq_count, tok_rows, query_heads, HEAD_WIDTH),
            cosine_table,
            -sine_table,
        )
        .reshape(flat_rows, -1)
        .astype(bf16)
    )
    grad_normed_part = jnp.dot(grad_q_b, wq_all.T, preferred_element_type=f32) + jnp.dot(
        grad_kv_b, wkv_flat.T, preferred_element_type=f32
    )
    grad_normed_part = (
        grad_normed_part
        + jnp.dot(grad_zx_b, wzx_flat.T, preferred_element_type=f32)
        + jnp.dot(grad_step_b, wdt_all.T, preferred_element_type=f32)
    )
    grad_normed = head_total(grad_normed_part) + jnp.dot(
        grad_bc_b, wbc_all.T, preferred_element_type=f32
    )
    _unused_in, in_pull = jax.vjp(rms_norm, residual, gain_in32)
    grad_resid_norm, grad_gain_in = in_pull(grad_normed)
    grad_tokens = (grad_mid + grad_resid_norm).reshape(seq_count, tok_rows, width_all)
    grad_q_w = jnp.dot(normed_b.T, grad_q_b, preferred_element_type=f32)
    grad_kv_w = jnp.dot(normed_b.T, grad_kv_b, preferred_element_type=f32).reshape(wkv_all.shape)
    grad_zx_w = jnp.dot(normed_b.T, grad_zx_b, preferred_element_type=f32).reshape(wzx_all.shape)
    grad_bc_w = jnp.dot(normed_b.T, grad_bc_b, preferred_element_type=f32)
    grad_dt_w = jnp.dot(normed_b.T, grad_step_b, preferred_element_type=f32)
    grad_list = (
        grad_gain_in,
        grad_gain_ff,
        grad_q_w,
        grad_kv_w,
        grad_o_w,
        grad_zx_w,
        grad_bc_w,
        grad_dt_w,
        grad_out_w,
        grad_gu_w,
        grad_down,
    )
    row_parts = (
        lax.psum_scatter(
            grad_list[0].astype(jnp.bfloat16), "fsdp", scatter_dimension=0, tiled=True
        ).astype(jnp.float32),
        *tuple(
            (
                part.astype(jnp.float32)
                for part in sent_together(
                    (
                        grad_list[1].astype(jnp.bfloat16),
                        grad_list[2].astype(jnp.bfloat16),
                        grad_list[3].astype(jnp.bfloat16),
                    ),
                    "fsdp",
                    0,
                    1,
                )
            )
        ),
        lax.psum_scatter(
            grad_list[4].astype(jnp.bfloat16), "fsdp", scatter_dimension=1, tiled=True
        ).astype(jnp.float32),
        *tuple(
            (
                part.astype(jnp.float32)
                for part in sent_together(
                    (
                        grad_list[5].astype(jnp.bfloat16),
                        grad_list[6].astype(jnp.bfloat16),
                        grad_list[7].astype(jnp.bfloat16),
                    ),
                    "fsdp",
                    0,
                    1,
                )
            )
        ),
        lax.psum_scatter(
            grad_list[8].astype(jnp.bfloat16), "fsdp", scatter_dimension=1, tiled=True
        ).astype(jnp.float32),
        lax.psum_scatter(
            grad_list[9].astype(jnp.bfloat16), "fsdp", scatter_dimension=0, tiled=True
        ).astype(jnp.float32),
        lax.psum_scatter(
            grad_list[10].astype(jnp.bfloat16), "fsdp", scatter_dimension=1, tiled=True
        ).astype(jnp.float32),
    )
    shard_list = (
        taken_together(row_parts[0].astype(jnp.bfloat16), "ctx").astype(jnp.float32),
        taken_together(row_parts[1].astype(jnp.bfloat16), "ctx").astype(jnp.float32),
        taken_together(row_parts[2].astype(jnp.bfloat16), "ctx").astype(jnp.float32),
        taken_together(row_parts[3].astype(jnp.bfloat16), "ctx").astype(jnp.float32),
        taken_together(row_parts[4].astype(jnp.bfloat16), "ctx").astype(jnp.float32),
        taken_together(row_parts[5].astype(jnp.bfloat16), "ctx").astype(jnp.float32),
        taken_together(row_parts[6].astype(jnp.bfloat16), "ctx").astype(jnp.float32),
        taken_together(row_parts[7].astype(jnp.bfloat16), "ctx").astype(jnp.float32),
        taken_together(row_parts[8].astype(jnp.bfloat16), "ctx").astype(jnp.float32),
        taken_together(row_parts[9].astype(jnp.bfloat16), "ctx").astype(jnp.float32),
        taken_together(row_parts[10].astype(jnp.bfloat16), "ctx").astype(jnp.float32),
    )
    small_total = together(
        (
            grad_taps[:, :inner_width],
            grad_taps[:, inner_width:],
            grad_decay_log,
            grad_step_bias,
            grad_skip,
        ),
        ("fsdp", "ctx"),
    )
    shard_list = tuple(shard_list)
    return (result, grad_tokens) + shard_list[:8] + tuple(small_total) + shard_list[8:]


def solution(mesh):
    return jax.shard_map(
        shards,
        mesh=mesh,
        in_specs=(
            P("fsdp", "ctx", None),
            P("fsdp", None),
            P("fsdp", "ctx", None),
            P("fsdp"),
            P("fsdp"),
            P("fsdp", "tp"),
            P("fsdp", None, "tp"),
            P("tp", "fsdp"),
            P("fsdp", None, "tp"),
            P("fsdp", None),
            P("fsdp", "tp"),
            P(None, "tp"),
            P(),
            P("tp"),
            P("tp"),
            P("tp"),
            P("tp", "fsdp"),
            P("fsdp", None, "tp"),
            P("tp", "fsdp"),
        ),
        out_specs=(
            P("fsdp", "ctx", None),
            P("fsdp", "ctx", None),
            P("fsdp"),
            P("fsdp"),
            P("fsdp", "tp"),
            P("fsdp", None, "tp"),
            P("tp", "fsdp"),
            P("fsdp", None, "tp"),
            P("fsdp", None),
            P("fsdp", "tp"),
            P(None, "tp"),
            P(),
            P("tp"),
            P("tp"),
            P("tp"),
            P("tp", "fsdp"),
            P("fsdp", None, "tp"),
            P("tp", "fsdp"),
        ),
        check_vma=False,
    )
```

profile of v0, /device:TPU:0, one launch (start us, length us, event | category | flops | bytes accessed | tf_op | source)
XLA Modules:
  0.0 1037.4 jit_solution(11413185915035106985)
XLA Ops:
  27.3 53.7 %all-gather.2.cloned.1.call-done = bf16[1024,6286]{1,0:T(8,128)(2,1)} async-done(((bf16[32,6286]{1,0:T(8,128)(2,1)}), bf16[1024,6286]{1,0:T(8,128)(2,1)}) %all-gather.2.cloned.1.call-update) | async-done | bytes 12873744 | tf_op jit(solution)/shard_map/all_gather | solution.py:31
  92.0 3.9 fusion.92
  162.5 89.2 %while.68 = (s32[]{:T(128)}, f32[12,64,128]{2,1,0:T(8,128)S(1)}, s32[]{:T(128)}, f32[4,128,12,64]{1,0,3,2:T(4,128)}, f32[4,128,12]{2,1,0:T(8,128)}, /*index=5*/s...) while((s32[]{:T(128)}, f32[12,64,128]{2,1,0:T(8,128)S(1)}, ...), condition=%wide.region_7.8_spmd, body=%wide.region_5.7_spmd.sunk | while | flops 479481216 | bytes 4469385 | solution.py:201
  170.5 10.7 %dynamic_update_slice.119 = f32[4,128,12,64]{1,0,3,2:T(4,128)} dynamic-update-slice(f32[4,128,12,64]{1,0,3,2:T(4,128)} %get-tuple-element.1434, f32[1,128,12,64]{1,0,3,2:T(1,128)} %bitcast.675, s32[]{:T(128)} %get-tuple-element.1431, s32[]{:T(128)} %constant.339.clone.1..sunk, s32[]{:T(128)} %constant.339.clone.1..sunk, s32[]{:T(128)} %constant.339.clone.1..sunk) | dynamic-update-slice | bytes 786436 | tf_op jit(solution)/shard_map/while/body/eval_jaxpr/while/body/jit(dynamic_update_index_in_dim)/dynamic_update_slice | solution.py:201
  192.9 10.7 %dynamic_update_slice.119 = f32[4,128,12,64]{1,0,3,2:T(4,128)} dynamic-update-slice(f32[4,128,12,64]{1,0,3,2:T(4,128)} %get-tuple-element.1434, f32[1,128,12,64]{1,0,3,2:T(1,128)} %bitcast.675, s32[]{:T(128)} %get-tuple-element.1431, s32[]{:T(128)} %constant.339.clone.1..sunk, s32[]{:T(128)} %constant.339.clone.1..sunk, s32[]{:T(128)} %constant.339.clone.1..sunk) | dynamic-update-slice | bytes 786436 | tf_op jit(solution)/shard_map/while/body/eval_jaxpr/while/body/jit(dynamic_update_index_in_dim)/dynamic_update_slice | solution.py:201
  215.2 10.7 %dynamic_update_slice.119 = f32[4,128,12,64]{1,0,3,2:T(4,128)} dynamic-update-slice(f32[4,128,12,64]{1,0,3,2:T(4,128)} %get-tuple-element.1434, f32[1,128,12,64]{1,0,3,2:T(1,128)} %bitcast.675, s32[]{:T(128)} %get-tuple-element.1431, s32[]{:T(128)} %constant.339.clone.1..sunk, s32[]{:T(128)} %constant.339.clone.1..sunk, s32[]{:T(128)} %constant.339.clone.1..sunk) | dynamic-update-slice | bytes 786436 | tf_op jit(solution)/shard_map/while/body/eval_jaxpr/while/body/jit(dynamic_update_index_in_dim)/dynamic_update_slice | solution.py:201
  237.5 10.7 %dynamic_update_slice.119 = f32[4,128,12,64]{1,0,3,2:T(4,128)} dynamic-update-slice(f32[4,128,12,64]{1,0,3,2:T(4,128)} %get-tuple-element.1434, f32[1,128,12,64]{1,0,3,2:T(1,128)} %bitcast.675, s32[]{:T(128)} %get-tuple-element.1431, s32[]{:T(128)} %constant.339.clone.1..sunk, s32[]{:T(128)} %constant.339.clone.1..sunk, s32[]{:T(128)} %constant.339.clone.1..sunk) | dynamic-update-slice | bytes 786436 | tf_op jit(solution)/shard_map/while/body/eval_jaxpr/while/body/jit(dynamic_update_index_in_dim)/dynamic_update_slice | solution.py:201
  266.2 53.2 %all_to_all.104 = f32[2,512,1024]{2,1,0:T(8,128)} all-to-all(f32[2,512,1024]{2,1,0:T(8,128)S(1)} %broadcast_in_dim.589), channel_id=1, replica_groups=mesh['fsdp'=32,'ctx'=2,'tp'=2] {'tp'}, dimensions={0} | all-to-all | bytes 8388608 | tf_op jit(solution)/shard_map/all_to_all | solution.py:19
  322.9 5.0 fusion.83
  327.9 4.8 fusion.111
  332.7 5.5 fusion.81
  340.8 5.6 all-to-all-start.4
  347.4 47.2 %all-to-all-done.4 = f32[2,512,1024]{2,1,0:T(8,128)} async-done(((f32[2,512,1024]{2,1,0:T(8,128)}), f32[2,512,1024]{2,1,0:T(8,128)}, u32[]{:S(2)}, u32[]{:S(2)}) %all-to-all-start.4) | async-done | bytes 4194336 | tf_op jit(solution)/shard_map/all_to_all | solution.py:19
  394.6 4.1 reduce_sum.545
  408.3 5.3 fusion.69
  435.8 4.2 convolution_convert_fusion.2
  440.1 4.1 convolution_convert_fusion.3
  444.2 52.3 %while.69 = (s32[]{:T(128)}, f32[12,64,128]{2,1,0:T(8,128)S(1)}, s32[]{:T(128)}, f32[4,12,64,128]{3,2,1,0:T(8,128)}, s32[4]{0:T(128)}, /*index=5*/f32[4,128,12]{...) while((s32[]{:T(128)}, f32[12,64,128]{2,1,0:T(8,128)S(1)}, ...), condition=%wide.region_16.17_spmd, body=%wide.region_14.16_spmd.sunk | while | flops 151488400 | bytes 2091625 | solution.py:201
  499.6 3.9 copy.480
  503.5 6.2 convolution_convert_fusion
  511.3 6.8 fusion.120
  525.4 148.7 %while.70 = (s32[]{:T(128)}, f32[12,64,128]{2,1,0:T(8,128)S(1)}, f32[4,128,12,64]{1,0,3,2:T(4,128)}, f32[4,128,128]{2,1,0:T(8,128)}, f32[4,128,128]{2,1,0:T(8,12...) while((s32[]{:T(128)}, f32[12,64,128]{2,1,0:T(8,128)S(1)}, ...), condition=%wide.region_27.28_spmd.clone, body=%wide.region_17.27_spmd.clone.sunk | while | flops 1136676736 | bytes 13674951 | solution.py:201
  550.0 10.7 %dynamic_update_slice.125 = f32[4,128,12,64]{1,0,3,2:T(4,128)} dynamic-update-slice(f32[4,128,12,64]{1,0,3,2:T(4,128)} %get-tuple-element.1508, f32[1,128,12,64]{1,0,3,2:T(1,128)S(1)} %bitcast.674, s32[]{:T(128)S(6)} %sub.384, s32[]{:T(128)} %constant.339.clone.1..sunk.1, s32[]{:T(128)} %constant.339.clone.1..sunk.1, s32[]{:T(128)} %constant.339.clone.1..sunk.1) | dynamic-update-slice | bytes 786436 | tf_op jit(solution)/shard_map/while/body/eval_jaxpr/transpose(jvp())/while/body/jit(dynamic_update_index_in_dim)/dynamic_update_slice | solution.py:201
  587.1 10.7 %dynamic_update_slice.125 = f32[4,128,12,64]{1,0,3,2:T(4,128)} dynamic-update-slice(f32[4,128,12,64]{1,0,3,2:T(4,128)} %get-tuple-element.1508, f32[1,128,12,64]{1,0,3,2:T(1,128)S(1)} %bitcast.674, s32[]{:T(128)S(6)} %sub.384, s32[]{:T(128)} %constant.339.clone.1..sunk.1, s32[]{:T(128)} %constant.339.clone.1..sunk.1, s32[]{:T(128)} %constant.339.clone.1..sunk.1) | dynamic-update-slice | bytes 786436 | tf_op jit(solution)/shard_map/while/body/eval_jaxpr/transpose(jvp())/while/body/jit(dynamic_update_index_in_dim)/dynamic_update_slice | solution.py:201
  624.1 10.7 %dynamic_update_slice.125 = f32[4,128,12,64]{1,0,3,2:T(4,128)} dynamic-update-slice(f32[4,128,12,64]{1,0,3,2:T(4,128)} %get-tuple-element.1508, f32[1,128,12,64]{1,0,3,2:T(1,128)S(1)} %bitcast.674, s32[]{:T(128)S(6)} %sub.384, s32[]{:T(128)} %constant.339.clone.1..sunk.1, s32[]{:T(128)} %constant.339.clone.1..sunk.1, s32[]{:T(128)} %constant.339.clone.1..sunk.1) | dynamic-update-slice | bytes 786436 | tf_op jit(solution)/shard_map/while/body/eval_jaxpr/transpose(jvp())/while/body/jit(dynamic_update_index_in_dim)/dynamic_update_slice | solution.py:201
  661.2 10.7 %dynamic_update_slice.125 = f32[4,128,12,64]{1,0,3,2:T(4,128)} dynamic-update-slice(f32[4,128,12,64]{1,0,3,2:T(4,128)} %get-tuple-element.1508, f32[1,128,12,64]{1,0,3,2:T(1,128)S(1)} %bitcast.674, s32[]{:T(128)S(6)} %sub.384, s32[]{:T(128)} %constant.339.clone.1..sunk.1, s32[]{:T(128)} %constant.339.clone.1..sunk.1, s32[]{:T(128)} %constant.339.clone.1..sunk.1) | dynamic-update-slice | bytes 786436 | tf_op jit(solution)/shard_map/while/body/eval_jaxpr/transpose(jvp())/while/body/jit(dynamic_update_index_in_dim)/dynamic_update_slice | solution.py:201
  675.0 4.3 all-to-all-start.5
  679.4 4.9 fusion.117
  693.6 4.6 all-to-all-start.6
  698.3 5.1 multiply_reduce_fusion.10
  703.9 5.0 reduce-window.16
  716.1 5.7 all-to-all-start.3
  724.1 4.4 multiply_reduce_fusion.5
  732.4 34.3 %collective-permute-done.3 = f32[1,3,1024]{2,1,0:T(4,128)S(1)} collective-permute-done((f32[1,3,1024]{2,1,0:T(4,128)S(1)}, f32[1,3,1024]{2,1,0:T(4,128)S(1)}, u32[]{:S(2)}, u32[]{:S(2)}) %collective-permute-start.3) | collective-permute-done | bytes 12320 | tf_op jit(solution)/shard_map/ppermute | solution.py:42
  775.2 6.2 copy.483
  796.6 3.6 all-to-all-done.19
  818.8 3.8 all-to-all-done.10
  824.2 5.9 all-to-all-start.16
  835.9 5.3 fusion.90
  841.2 7.4 all-to-all-done.16
  853.5 4.1 add_add_fusion.3
  860.4 6.1 all-to-all-start.7
  867.7 4.2 reduce_sum.543
  882.7 32.7 %all-to-all-done.7 = f32[2,512,1024]{2,1,0:T(8,128)} async-done(((f32[2,512,1024]{2,1,0:T(8,128)}), f32[2,512,1024]{2,1,0:T(8,128)}, u32[]{:S(2)}, u32[]{:S(2)}) %all-to-all-start.7) | async-done | bytes 4194336 | tf_op jit(solution)/shard_map/all_to_all | solution.py:19
  915.5 4.1 reduce_sum.554
  919.6 4.2 fusion.97
  923.8 63.4 %all-reduce.12 = bf16[1024]{0:T(1024)(128)(2,1)S(1)} all-reduce(bf16[1024]{0:T(1024)(128)(2,1)S(1)} %get-tuple-element.1019), channel_id=2, replica_groups=mesh['fsdp'=32,'ctx'=2,'tp'=2] {'fsdp'}, use_global_device_ids=true, to_apply=%region_38.39.clone | all-reduce | flops 1024 | bytes 4096
  1025.1 4.2 all-to-all-done.13
  (854 shorter events, 489.7 us)
Async XLA Ops:
  7.2 73.8 %all-gather.2.cloned.1.call-start = ((), (), s32[]{:S(2)}) async-start(), calls=%async_computation.26 | async-start | bytes 13516800 | tf_op jit(solution)/shard_map/all_gather | solution.py:31
  21.3 63.4 %copy-start.119 = (f32[32]{0:T(128)}, f32[32]{0:T(128)S(1)}, u32[]{:S(2)}) copy-start(f32[32]{0:T(128)S(1)} %multiply_exponential_fusion) | copy-start | bytes 388
  21.3 63.4 %copy-start.92 = (f32[512]{0:T(512)}, f32[512]{0:T(512)S(1)}, u32[]{:S(2)}) copy-start(f32[512]{0:T(512)S(1)} %fusion.228) | copy-start | bytes 6148
  22.4 63.2 %copy-start.109 = (f32[512]{0:T(512)}, f32[512]{0:T(512)S(1)}, u32[]{:S(2)}) copy-start(f32[512]{0:T(512)S(1)} %fusion.100) | copy-start | bytes 6148
  23.0 78.2 %copy-start.105 = (f32[512]{0:T(512)}, f32[512]{0:T(512)S(1)}, u32[]{:S(2)}) copy-start(f32[512]{0:T(512)S(1)} %fusion.226) | copy-start | bytes 6148
  24.9 103.7 %copy-start.76 = (f32[1,1024]{1,0:T(1,128)}, f32[1,1024]{1,0:T(1,128)S(1)}, u32[]{:S(2)}) copy-start(f32[1,1024]{1,0:T(1,128)S(1)} %get-tuple-element.1141) | copy-start | bytes 12292
  24.9 103.7 %copy-start.78 = (f32[1,1024]{1,0:T(1,128)}, f32[1,1024]{1,0:T(1,128)S(1)}, u32[]{:S(2)}) copy-start(f32[1,1024]{1,0:T(1,128)S(1)} %get-tuple-element.1142) | copy-start | bytes 12292
  24.9 103.7 %copy-start.80 = (f32[1,1024]{1,0:T(1,128)}, f32[1,1024]{1,0:T(1,128)S(1)}, u32[]{:S(2)}) copy-start(f32[1,1024]{1,0:T(1,128)S(1)} %get-tuple-element.1143) | copy-start | bytes 12292
  25.9 97.9 %copy-start.51 = (f32[512,32]{0,1:T(8,128)}, f32[512,32]{0,1:T(8,128)S(1)}, u32[]{:S(2)}) copy-start(f32[512,32]{0,1:T(8,128)S(1)} %get-tuple-element.1152) | copy-start | bytes 196612
  85.7 69.8 %copy-start.35 = (bf16[512,128]{0,1:T(8,128)(2,1)}, bf16[512,128]{0,1:T(8,128)(2,1)S(1)}, u32[]{:S(2)}) copy-start(bf16[512,128]{0,1:T(8,128)(2,1)S(1)} %get-tuple-element.1134) | copy-start | bytes 393220
  85.7 65.9 %collective-permute-start = (bf16[1,512,128]{1,2,0:T(8,128)(2,1)}, bf16[1,512,128]{1,2,0:T(8,128)(2,1)S(1)}, u32[]{:S(2)}, u32[]{:S(2)}) collective-permute-start(bf16[1,512,128]{1,2,0:T(8,128)(2,1)} %get-tuple-element.1133), channel_id=1, source_target_pairs={{0,2},{1,3},{4,6},{5,7},{8,10},{9,11},{12,14},{13,15},{16,18},{17,... | collective-permute-start | bytes 393224 | tf_op jit(solution)/shard_map/ppermute | solution.py:42
  99.3 28.3 %collective-permute-start.1 = (f32[1,3,1024]{2,1,0:T(4,128)}, f32[1,3,1024]{2,1,0:T(4,128)}, u32[]{:S(2)}, u32[]{:S(2)}) collective-permute-start(f32[1,3,1024]{2,1,0:T(4,128)} %slice.447), channel_id=1, source_target_pairs={{0,2},{1,3},{4,6},{5,7},{8,10},{9,11},{12,14},{13,15},{16,18},{17,... | collective-permute-start | bytes 36872 | tf_op jit(solution)/shard_map/ppermute | solution.py:42
  118.7 7.1 all-to-all-start
  146.2 13.7 %all-to-all-start.1 = ((bf16[2,1,12,64,128]{4,3,2,1,0:T(8,128)(2,1)}), bf16[2,1,12,64,128]{4,3,2,1,0:T(8,128)(2,1)S(1)}, u32[]{:S(2)}, u32[]{:S(2)}) async-start(bf16[2,1,12,64,128]{4,3,2,1,0:T(8,128)(2,1)} %broadcast_in_dim.586), calls=%async_computation.1 | async-start | bytes 786432 | tf_op jit(solution)/shard_map/all_to_all | solution.py:19
  322.1 181.4 %copy-start.3 = (f32[512,1024]{1,0:T(8,128)}, f32[512,1024]{1,0:T(8,128)S(1)}, u32[]{:S(2)}) copy-start(f32[512,1024]{1,0:T(8,128)S(1)} %reduce_sum.540) | copy-start | bytes 6291460
  340.8 53.7 %all-to-all-start.4 = ((f32[2,512,1024]{2,1,0:T(8,128)}), f32[2,512,1024]{2,1,0:T(8,128)}, u32[]{:S(2)}, u32[]{:S(2)}) async-start(f32[2,512,1024]{2,1,0:T(8,128)} %broadcast_in_dim.591), calls=%async_computation.4 | async-start | bytes 8388608 | tf_op jit(solution)/shard_map/all_to_all | solution.py:19
  346.5 435.9 %reduce-scatter.11.cloned.1.call-start = ((), (), s32[]{:S(2)}) async-start(), calls=%async_computation.27 | async-start | bytes 540672 | tf_op jit(solution)/shard_map/reduce_scatter | solution.py:634
  421.9 365.1 %reduce-scatter.19.cloned.1.call-start = ((), (), s32[]{:S(2)}) async-start(), calls=%async_computation.31 | async-start | bytes 1081344
  423.1 6.9 collective-permute-start.2
  435.5 355.4 %reduce-scatter.17.cloned.1.call-start = ((), (), s32[]{:S(2)}) async-start(), calls=%async_computation.30 | async-start | bytes 2162688 | tf_op jit(solution)/shard_map/reduce_scatter | solution.py:658
  440.0 408.6 %reduce-scatter.13.cloned.1.call-start = ((), (), s32[]{:S(2)}) async-start(), calls=%async_computation.28 | async-start | bytes 1622016 | tf_op jit(solution)/shard_map/reduce_scatter | solution.py:652
  444.2 551.1 %reduce-scatter.15.cloned.1.call-start = ((), (), s32[]{:S(2)}) async-start(), calls=%async_computation.29 | async-start | bytes 4325376 | tf_op jit(solution)/shard_map/reduce_scatter | solution.py:655
  675.0 14.6 %all-to-all-start.5 = ((bf16[2,1,12,64,128]{4,3,2,1,0:T(8,128)(2,1)}), bf16[2,1,12,64,128]{4,3,2,1,0:T(8,128)(2,1)}, u32[]{:S(2)}, u32[]{:S(2)}) async-start(bf16[2,1,12,64,128]{4,3,2,1,0:T(8,128)(2,1)} %broadcast_in_dim.596), calls=%async_computation.5 | async-start | bytes 786432 | tf_op jit(solution)/shard_map/all_to_all | solution.py:19
  693.6 20.0 %all-to-all-start.6 = ((f32[2,1,512,256]{3,2,1,0:T(8,128)}), f32[2,1,512,256]{3,2,1,0:T(8,128)}, u32[]{:S(2)}, u32[]{:S(2)}) async-start(f32[2,1,512,256]{3,2,1,0:T(8,128)} %broadcast_in_dim.601), calls=%async_computation.6 | async-start | bytes 2097152 | tf_op jit(solution)/shard_map/all_to_all | solution.py:19
  716.1 66.2 %all-to-all-start.3 = ((f32[2,512,1024]{2,1,0:T(8,128)}), f32[2,512,1024]{2,1,0:T(8,128)}, u32[]{:S(2)}, u32[]{:S(2)}) async-start(f32[2,512,1024]{2,1,0:T(8,128)} %broadcast_in_dim.590), calls=%async_computation.3 | async-start | bytes 8388608 | tf_op jit(solution)/shard_map/all_to_all | solution.py:19
  721.8 278.5 %reduce-scatter.21.cloned.1.call-start = ((), (), s32[]{:S(2)}) async-start(), calls=%async_computation.32 | async-start | bytes 4055040
  729.2 37.4 %collective-permute-start.3 = (f32[1,3,1024]{2,1,0:T(4,128)S(1)}, f32[1,3,1024]{2,1,0:T(4,128)S(1)}, u32[]{:S(2)}, u32[]{:S(2)}) collective-permute-start(f32[1,3,1024]{2,1,0:T(4,128)S(1)} %add_bitcast_fusion.2), channel_id=1, source_target_pairs={{2,0},{3,1},{6,4},{7,5},{10,8},{11,9},{14,12},{15,13},{18,16},{19,... | collective-permute-start | bytes 36872 | tf_op jit(solution)/shard_map/ppermute | solution.py:42
  732.4 35.4 %copy-start.47 = (bf16[512,768]{1,0:T(8,128)(2,1)S(1)}, bf16[512,768]{1,0:T(8,128)(2,1)}, u32[]{:S(2)}) copy-start(bf16[512,768]{1,0:T(8,128)(2,1)} %get-tuple-element.1112) | copy-start | bytes 2359300
  781.5 37.2 %copy-start.126 = (f32[12]{0:T(128)S(1)}, f32[12]{0:T(128)}, u32[]{:S(2)}) copy-start(f32[12]{0:T(128)} %get-tuple-element.1094) | copy-start | bytes 148
  783.7 7.2 all-to-all-start.12
  788.0 42.1 %copy-start.53 = (bf16[512,64]{0,1:T(8,128)(2,1)S(1)}, bf16[512,64]{0,1:T(8,128)(2,1)}, u32[]{:S(2)}) copy-start(bf16[512,64]{0,1:T(8,128)(2,1)} %copy-done.52) | copy-start | bytes 196612
  788.0 42.1 %copy-start.55 = (bf16[512,64]{0,1:T(8,128)(2,1)S(1)}, bf16[512,64]{0,1:T(8,128)(2,1)}, u32[]{:S(2)}) copy-start(bf16[512,64]{0,1:T(8,128)(2,1)} %copy-done.54) | copy-start | bytes 196612
  792.4 7.8 all-to-all-start.19
  800.8 6.9 all-to-all-start.9
  807.7 7.1 all-to-all-start.11
  815.4 7.2 all-to-all-start.10
  824.2 24.4 %all-to-all-start.16 = ((f32[64,1,4132]{2,1,0:T(1,128)}), f32[64,1,4132]{2,1,0:T(1,128)S(1)}, u32[]{:S(2)}, u32[]{:S(2)}) async-start(f32[64,1,4132]{2,1,0:T(1,128)} %broadcast_in_dim.619), calls=%async_computation.17 | async-start | bytes 2162688 | tf_op jit(solution)/shard_map/all_to_all | solution.py:19
  850.1 7.6 all-to-all-start.17
  860.4 55.1 %all-to-all-start.7 = ((f32[2,512,1024]{2,1,0:T(8,128)}), f32[2,512,1024]{2,1,0:T(8,128)}, u32[]{:S(2)}, u32[]{:S(2)}) async-start(f32[2,512,1024]{2,1,0:T(8,128)} %broadcast_in_dim.605), calls=%async_computation.7 | async-start | bytes 8388608 | tf_op jit(solution)/shard_map/all_to_all | solution.py:19
  882.7 36.9 %copy-start.91 = (f32[1024]{0:T(1024)S(1)}, f32[1024]{0:T(1024)}, u32[]{:S(2)}) copy-start(f32[1024]{0:T(1024)} %copy-done.88) | copy-start | bytes 12292
  882.7 36.9 %copy-start.108 = (f32[512]{0:T(512)S(1)}, f32[512]{0:T(512)}, u32[]{:S(2)}) copy-start(f32[512]{0:T(512)} %copy-done.105) | copy-start | bytes 6148
  919.6 71.5 %copy-start.110 = (f32[512]{0:T(512)S(1)}, f32[512]{0:T(512)}, u32[]{:S(2)}) copy-start(f32[512]{0:T(512)} %copy-done.109) | copy-start | bytes 6148
  919.6 71.5 %copy-start.11 = (f32[512,1024]{1,0:T(8,128)S(1)}, f32[512,1024]{1,0:T(8,128)}, u32[]{:S(2)}) copy-start(f32[512,1024]{1,0:T(8,128)} %fusion.98) | copy-start | bytes 6291460
  987.9 6.9 all-to-all-start.8
  996.9 8.6 all-to-all-start.18
  1005.5 7.0 all-to-all-start.15
  1013.1 7.2 all-to-all-start.14
  1021.0 8.2 all-to-all-start.13
  (135 other events, 783.6 us)
Sparse Core Ops, SparseCore 0:
  14.4 66.5 all-gather.1
  422.1 75.1 reduce-scatter.10
  500.7 76.9 reduce-scatter.18
  581.5 78.2 reduce-scatter.16
  663.6 77.5 reduce-scatter.12
  745.2 81.3 reduce-scatter.14
  830.2 81.0 reduce-scatter.20
where the time goes:
time: 1050 us; the launch traced here: 1040 us
  local copies, waits for them, and re-layouts  274 us (26%)
  waiting for transfers between devices  208 us (20%)
  matrix products  189 us (18%)
  other arithmetic  141 us (13%)
  blocking collectives  117 us (11%)
  starting transfers between devices  84 us (8%)
  between operations  19.1 us (2%)
    all_to_all x19, waiting for transfers between devices, sent_to_all(): lax.all_to_all(jnp.broadcast_to(array[None], (devices, *array.shape)), ax...  117 us
    dynamic_update_slice x20, local copies, waits for them, and re-layouts, ssd_scan(): lax.scan(jax.checkpoint(span_step), (state_start, seg_before), pieces)  96.2 us
    all_to_all x19, starting transfers between devices, sent_to_all(): lax.all_to_all(jnp.broadcast_to(array[None], (devices, *array.shape)), ax...  75.3 us
    unnamed x1, blocking collectives  63.4 us
    all_gather x1, waiting for transfers between devices, turned_gather(): lax.all_gather(both, axis, axis=0, tiled=True)  53.7 us
    all_to_all x1, blocking collectives, sent_to_all(): lax.all_to_all(jnp.broadcast_to(array[None], (devices, *array.shape)), ax...  53.2 us
    ppermute x4, waiting for transfers between devices, passed_along(): return lax.ppermute(block, axis, route)  37.3 us
    unnamed x299, local copies, waits for them, and re-layouts  29 us
  transfers between devices with their start and end apart: 30, of which 18 were waited for; matrix products, arithmetic and copies ran while one was open for 41% of the time, Pallas kernels for 0%

commit v1 on v0

v1 whole, which is shorter than its diff:
```python
import functools
import math

import jax
import jax.numpy as jnp
from jax import lax
from jax.experimental import pallas as pl
from jax.experimental.pallas import tpu as pltpu
from jax.sharding import Mesh
from jax.sharding import PartitionSpec as P

f32 = jnp.float32
bf16 = jnp.bfloat16
EPS = 1e-05
NEG = -1e30
ROPE_BASE = 100000000000.0
HEAD_WIDTH = 64
HIGH = lax.Precision.HIGHEST

TOK = 512
WID = 1024
SPAN = 128
SPANS = TOK // SPAN
QW = 256
HEADS = 12
INNER = 768
STATE = 128
CONV = INNER + 2 * STATE
HALO = 16
W1C = 2304
W2C = 1024
W3C = 3072
FFH = 1024
C_Q, C_KV, C_DT, C_Z, C_U = 0, 256, 384, 512, 1280


def vmem(n):
    return [pl.BlockSpec(memory_space=pltpu.VMEM)] * n


def kernel_call(body, outs, scratch=(), mem=56, cost=None):
    def call(*args):
        return pl.pallas_call(
            body,
            out_shape=[jax.ShapeDtypeStruct(s, d) for s, d in outs],
            in_specs=vmem(len(args)),
            out_specs=vmem(len(outs)),
            scratch_shapes=list(scratch),
            compiler_params=pltpu.CompilerParams(vmem_limit_bytes=mem * 1024 * 1024),
            cost_estimate=cost,
        )(*args)

    return call


def nt(a, b):
    return lax.dot_general(a, b, (((1,), (1,)), ((), ())), preferred_element_type=f32)


def tn(a, b):
    return lax.dot_general(a, b, (((0,), (0,)), ((), ())), preferred_element_type=f32)


def nn(a, b):
    return jnp.dot(a, b, preferred_element_type=f32)


def split_halves(v):
    hi = v.astype(bf16)
    return hi, (v - hi.astype(f32)).astype(bf16)


def head_matrix(rows, columns):
    row = lax.broadcasted_iota(jnp.int32, (rows, columns), 0)
    col = lax.broadcasted_iota(jnp.int32, (rows, columns), 1)
    return row, col


def spread(v):
    row, col = head_matrix(128, INNER)
    e = jnp.where(row == col // 64, 1.0, 0.0).astype(bf16)
    hi, lo = split_halves(v)
    return nn(hi, e) + nn(lo, e)


def gathered_heads(v):
    row, col = head_matrix(INNER, 128)
    e = jnp.where(row // 64 == col, 1.0, 0.0).astype(bf16)
    hi, lo = split_halves(v)
    return nn(hi, e) + nn(lo, e)


def low_half(shape):
    return lax.broadcasted_iota(jnp.int32, shape, len(shape) - 1) % 128 < 64


def sigmoid(v):
    return 1.0 / (1.0 + jnp.exp(-v))


def turned(v, cos, sin):
    lane = lax.broadcasted_iota(jnp.int32, v.shape, 1) % 64
    w = v.shape[1]
    swapped = jnp.where(lane < 32, pltpu.roll(v, w - 32, 1), pltpu.roll(v, 32, 1))
    return v * cos + jnp.where(lane < 32, -swapped, swapped) * sin


def unit_rows(v):
    r = lax.rsqrt(jnp.mean(v * v, axis=1, keepdims=True) + EPS)
    return v * r, r


def project_body(
    tok, prior, w1, gain, cos, sin, cosp, sinp, normed, q, k2, v2, k2p, v2p, z, cin, step, norm_p
):
    g = gain[...]
    normed[...] = (unit_rows(tok[...].astype(f32))[0] * g).astype(bf16)
    norm_p[...] = (unit_rows(prior[...].astype(f32))[0] * g).astype(bf16)
    lin = nn(normed[...], w1[:, 0:256])
    c, s = cos[...], sin[...]
    for i in range(2):
        cols = slice(128 * i, 128 * i + 128)
        q[:, cols] = turned(lin[:, cols], c, s).astype(bf16)
    low = low_half((TOK, 128))

    def pair(block, cc, ss, kk, vv):
        rot = turned(block, cc, ss)
        shifted = pltpu.roll(rot, 64, 1)
        kk[...] = jnp.where(low, rot, shifted).astype(bf16)
        flat = pltpu.roll(block, 64, 1)
        vv[...] = jnp.where(low, flat, block).astype(bf16)

    lin = nn(normed[...], w1[:, 256:512])
    pair(lin[:, 0:128], c, s, k2, v2)
    step[...] = lin[:, 128:256]
    pair(nn(norm_p[...], w1[:, 256:384]), cosp[...], sinp[...], k2p, v2p)

    @pl.loop(0, 3)
    def _(j):
        at = pl.ds(pl.multiple_of(C_Z + j * 256, 256), 256)
        to = pl.ds(pl.multiple_of(j * 256, 256), 256)
        z[:, to] = nn(normed[...], w1[:, at])

    @pl.loop(0, 4)
    def _(j):
        at = pl.ds(pl.multiple_of(C_U + j * 256, 256), 256)
        to = pl.ds(pl.multiple_of(j * 256, 256), 256)
        cin[0:HALO, to] = nn(norm_p[TOK - HALO : TOK, :], w1[:, at])
        cin[HALO : HALO + TOK, to] = nn(normed[...], w1[:, at])


project = kernel_call(
    project_body,
    [
        ((TOK, WID), bf16),
        ((TOK, QW), bf16),
        ((TOK, 128), bf16),
        ((TOK, 128), bf16),
        ((TOK, 128), bf16),
        ((TOK, 128), bf16),
        ((TOK, INNER), f32),
        ((HALO + TOK, CONV), f32),
        ((TOK, 128), f32),
    ],
    [pltpu.VMEM((TOK, WID), bf16)],
)


def own_bias(rows, start, seg_col, seg_row):
    end = start + rows
    query = lax.broadcasted_iota(jnp.int32, (rows, end), 0) + start
    key = lax.broadcasted_iota(jnp.int32, (rows, end), 1)
    keep = (key <= query) & (seg_col[start:end, 0:1] == seg_row[0:1, TOK : TOK + end])
    return keep


QB = 256


def attend_body(q, k2, v2, k2p, v2p, seg_col, seg_row, out, lse):
    low = low_half((QB, 128))
    for b in range(TOK // QB):
        start, end = b * QB, (b + 1) * QB
        keep = own_bias(QB, start, seg_col, seg_row)
        keep_p = seg_col[start:end, 0:1] == seg_row[0:1, 0:TOK]
        logs = []
        for pair in range(2):
            cols = slice(128 * pair, 128 * pair + 128)
            qp = q[start:end, cols]
            halves = []
            for side in range(2):
                mine = low if side == 0 else ~low
                qh = jnp.where(mine, qp.astype(f32) * 0.125, 0.0).astype(bf16)
                s1 = jnp.where(keep, nt(qh, k2[0:end, :]), NEG)
                s0 = jnp.where(keep_p, nt(qh, k2p[...]), NEG)
                m = jnp.maximum(
                    jnp.max(s1, axis=1, keepdims=True), jnp.max(s0, axis=1, keepdims=True)
                )
                p1, p0 = jnp.exp(s1 - m), jnp.exp(s0 - m)
                total = jnp.sum(p1, axis=1, keepdims=True) + jnp.sum(p0, axis=1, keepdims=True)
                o = nn(p1.astype(bf16), v2[0:end, :]) + nn(p0.astype(bf16), v2p[...])
                halves.append(o / total)
                logs.append(m + jnp.log(total))
            out[start:end, cols] = jnp.where(low, halves[0], halves[1]).astype(bf16)
        lane = lax.broadcasted_iota(jnp.int32, (QB, 128), 1)
        kept = jnp.zeros((QB, 128), f32)
        for h in range(4):
            kept = jnp.where(lane == h, logs[h], kept)
        lse[start:end, :] = kept


attend = kernel_call(attend_body, [((TOK, QW), bf16), ((TOK, 128), f32)])


def attend_back_body(
    q, k2, v2, k2p, v2p, seg_col, seg_row, lse, dout, cos, sin, dq, dkv, dkv_p, dk_s, dv_s, dkp_s, dvp_s
):
    low = low_half((QB, 128))
    for ref in (dk_s, dv_s, dkp_s, dvp_s):
        ref[...] = jnp.zeros_like(ref)
    for b in range(TOK // QB):
        start, end = b * QB, (b + 1) * QB
        keep = own_bias(QB, start, seg_col, seg_row)
        keep_p = seg_col[start:end, 0:1] == seg_row[0:1, 0:TOK]
        for pair in range(2):
            cols = slice(128 * pair, 128 * pair + 128)
            qp = q[start:end, cols]
            dop = dout[start:end, cols]
            halves = []
            for side in range(2):
                mine = low if side == 0 else ~low
                qh = jnp.where(mine, qp.astype(f32) * 0.125, 0.0).astype(bf16)
                doh = jnp.where(mine, dop.astype(f32), 0.0).astype(bf16)
                h = 2 * pair + side
                log_total = lse[start:end, h : h + 1]
                p1 = jnp.exp(jnp.where(keep, nt(qh, k2[0:end, :]), NEG) - log_total)
                p0 = jnp.exp(jnp.where(keep_p, nt(qh, k2p[...]), NEG) - log_total)
                dp1 = nt(doh, v2[0:end, :])
                dp0 = nt(doh, v2p[...])
                delta = jnp.sum(p1 * dp1, axis=1, keepdims=True) + jnp.sum(
                    p0 * dp0, axis=1, keepdims=True
                )
                ds1 = (p1 * (dp1 - delta)).astype(bf16)
                ds0 = (p0 * (dp0 - delta)).astype(bf16)
                dv_s[0:end, :] += tn(p1.astype(bf16), doh)
                dvp_s[...] += tn(p0.astype(bf16), doh)
                dk_s[0:end, :] += tn(ds1, qh)
                dkp_s[...] += tn(ds0, qh)
                halves.append(nn(ds1, k2[0:end, :]) + nn(ds0, k2p[...]))
            dqp = jnp.where(low, halves[0], halves[1]) * 0.125
            dq[start:end, cols] = turned(dqp, cos[start:end, :], -sin[start:end, :]).astype(bf16)
    low = low_half((TOK, 128))

    def joined(dk, dv):
        dk, dv = dk[...], dv[...]
        return jnp.where(low, dk + pltpu.roll(dk, 64, 1), dv + pltpu.roll(dv, 64, 1))

    dkv[...] = joined(dk_s, dv_s)
    dkv_p[...] = joined(dkp_s, dvp_s).astype(bf16)


attend_back = kernel_call(
    attend_back_body,
    [((TOK, QW), bf16), ((TOK, 128), f32), ((TOK, 128), bf16)],
    [pltpu.VMEM((TOK, 128), f32)] * 4,
)


def tap_mask(seg_ext, k):
    now = seg_ext[HALO : HALO + TOK, 0:1]
    at = HALO - 3 + k
    return jnp.where(seg_ext[at : at + TOK, 0:1] == now, 1.0, 0.0)


def lower_ones():
    row, col = head_matrix(SPAN, SPAN)
    return jnp.where(row >= col, 1.0, 0.0)


def rows_of(c):
    return slice(c * SPAN, (c + 1) * SPAN)


def mixer_in_body(cin, taps, step, bias, rate, seg_ext, pre, dt, cum, last):
    run = jnp.zeros((TOK, CONV), f32)
    for k in range(4):
        at = HALO - 3 + k
        run = run + cin[at : at + TOK, :] * taps[k : k + 1, :] * tap_mask(seg_ext, k)
    pre[...] = run
    lane = lax.broadcasted_iota(jnp.int32, (TOK, 128), 1)
    steps = step[...] + bias[...]
    soft = jnp.maximum(steps, 0.0) + jnp.log(1.0 + jnp.exp(-jnp.abs(steps)))
    dt[...] = jnp.where(lane < HEADS, soft, 0.0)
    tri = lower_ones()
    state = jnp.zeros((STATE, INNER), f32)
    for c in range(SPANS):
        rows = rows_of(c)
        own_dt = dt[rows, :]
        total = jnp.dot(tri, own_dt * rate[...], precision=HIGH, preferred_element_type=f32)
        cum[rows, :] = total
        out = pre[rows, 0 : INNER + STATE]
        out = out * sigmoid(out)
        seg = seg_ext[HALO + c * SPAN : HALO + (c + 1) * SPAN, 0:1]
        seg_last = seg[SPAN - 1 : SPAN, :]
        end = total[SPAN - 1 : SPAN, :]
        tail = jnp.where(seg == seg_last, jnp.exp(jnp.minimum(end - total, 0.0)), 0.0) * own_dt
        fresh = tn(out[:, INNER:].astype(bf16), (out[:, 0:INNER] * spread(tail)).astype(bf16))
        if c == 0:
            state = fresh
        else:
            seg_prev = seg_ext[HALO + c * SPAN - 1 : HALO + c * SPAN, 0:1]
            keep = jnp.where(seg_last == seg_prev, jnp.exp(end), 0.0)
            state = state * spread(jnp.broadcast_to(keep, (8, 128)))[0:1, :] + fresh
    last[...] = state.astype(bf16)


mixer_in = kernel_call(
    mixer_in_body,
    [
        ((TOK, CONV), f32),
        ((TOK, 128), f32),
        ((TOK, 128), f32),
        ((STATE, INNER), bf16),
    ],
)


def span_parts(c, cum, seg_ext):
    total = cum[rows_of(c), :]
    seg = seg_ext[HALO + c * SPAN : HALO + (c + 1) * SPAN, 0:1]
    seg_last = seg[SPAN - 1 : SPAN, :]
    seg_prev = seg_ext[HALO + c * SPAN - 1 : HALO + c * SPAN, 0:1]
    end = total[SPAN - 1 : SPAN, :]
    entering = jnp.where(seg == seg_prev, jnp.exp(total), 0.0)
    tail = jnp.where(seg == seg_last, jnp.exp(jnp.minimum(end - total, 0.0)), 0.0)
    return total, entering, tail


def span_bias(c, seg_ext, seg_row):
    row, col = head_matrix(SPAN, SPAN)
    seg = seg_ext[HALO + c * SPAN : HALO + (c + 1) * SPAN, 0:1]
    other = seg_row[0:1, TOK + c * SPAN : TOK + (c + 1) * SPAN]
    return jnp.where((row >= col) & (seg == other), 0.0, NEG)


def mixer_out_body(
    pre, dt, cum, seg_ext, seg_row, first, z, skip, y, gated, states, sc_state
):
    sc_state[...] = first[...].astype(f32)
    low2 = low_half((SPAN, 128))
    for c in range(SPANS):
        rows = rows_of(c)
        total, entering, tail = span_parts(c, cum, seg_ext)
        out = pre[rows, :]
        out = out * sigmoid(out)
        x = out[:, 0:INNER]
        b = out[:, INNER : INNER + STATE].astype(bf16)
        cm = out[:, INNER + STATE :].astype(bf16)
        own_dt = dt[rows, :]
        xs = x * spread(own_dt)
        state = sc_state[...]
        state_b = state.astype(bf16)
        states[c] = state_b
        wide_in = spread(entering)
        run = nn(cm, state_b) * wide_in + x * skip[...]
        inter = nt(cm, b)
        bias = span_bias(c, seg_ext, seg_row)
        total_t = total.T
        gate = z[rows, :]
        gate = gate * sigmoid(gate)
        for pair in range(HEADS // 2):
            cols = slice(128 * pair, 128 * pair + 128)
            parts = []
            for side in range(2):
                h = 2 * pair + side
                decay = jnp.exp(total[:, h : h + 1] - total_t[h : h + 1, :] + bias)
                parts.append((decay * inter).astype(bf16))
            xp = xs[:, cols]
            stack = jnp.concatenate(
                [jnp.where(low2, xp, 0.0).astype(bf16), jnp.where(low2, 0.0, xp).astype(bf16)], axis=0
            )
            yp = run[:, cols] + nn(jnp.concatenate(parts, axis=1), stack)
            y[rows, cols] = yp
            gated[rows, cols] = (yp * gate[:, cols]).astype(bf16)
        if c < SPANS - 1:
            sc_state[...] = state * wide_in[SPAN - 1 : SPAN, :] + tn(
                b, (xs * spread(tail)).astype(bf16)
            )


mixer_out = kernel_call(
    mixer_out_body,
    [((TOK, INNER), f32), ((TOK, INNER), bf16), ((SPANS, STATE, INNER), bf16)],
    [pltpu.VMEM((STATE, INNER), f32)],
)


def mixer_back_in_body(dgated, z, y, pre, cum, seg_ext, dy, dz, first):
    state = jnp.zeros((STATE, INNER), f32)
    for c in reversed(range(SPANS)):
        rows = rows_of(c)
        total, entering, tail = span_parts(c, cum, seg_ext)
        gate = z[rows, :]
        sig = sigmoid(gate)
        grad = dgated[rows, :]
        own = grad * (gate * sig)
        dy[rows, :] = own
        dz[rows, :] = (grad * y[rows, :] * (sig * (1.0 + gate * (1.0 - sig)))).astype(bf16)
        cm = pre[rows, INNER + STATE :]
        cm = (cm * sigmoid(cm)).astype(bf16)
        wide_in = spread(entering)
        fresh = tn(cm, (own * wide_in).astype(bf16))
        state = fresh if c == SPANS - 1 else state * wide_in[SPAN - 1 : SPAN, :] + fresh
    first[...] = state.astype(bf16)


mixer_back_in = kernel_call(
    mixer_back_in_body,
    [((TOK, INNER), f32), ((TOK, INNER), bf16), ((STATE, INNER), bf16)],
)


def mixer_back_body(
    dy, pre, dt, cum, seg_ext, seg_row, states, last, skip, rate, step, bias,
    dpre, dstep, heads, sc_state,
):
    sc_state[...] = last[...].astype(f32)
    low2 = low_half((SPAN, 128))
    lane = lax.broadcasted_iota(jnp.int32, (SPAN, 128), 1)
    tri = lower_ones()
    sum_decay = jnp.zeros((1, 128), f32)
    sum_bias = jnp.zeros((1, 128), f32)
    sum_skip = jnp.zeros((1, 128), f32)
    for c in reversed(range(SPANS)):
        rows = rows_of(c)
        total, entering, tail = span_parts(c, cum, seg_ext)
        lin = pre[rows, :]
        sig = sigmoid(lin)
        out = lin * sig
        slope = sig * (1.0 + lin * (1.0 - sig))
        x = out[:, 0:INNER]
        b = out[:, INNER : INNER + STATE].astype(bf16)
        cm = out[:, INNER + STATE :].astype(bf16)
        own_dt = dt[rows, :]
        wide_dt = spread(own_dt)
        xs = x * wide_dt
        grad = dy[rows, :]
        wide_in = spread(entering)
        wide_tail = spread(tail)
        dstate = sc_state[...]
        dstate_b = dstate.astype(bf16)
        state_b = states[c]
        gin = grad * wide_in
        gin_b = gin.astype(bf16)
        y_state = nn(cm, state_b)
        xt = xs * wide_tail
        xt_b = xt.astype(bf16)
        from_state = nn(b, dstate_b)
        dcm = nt(gin_b, state_b)
        db = nt(xt_b, dstate_b)
        dcum = gathered_heads(gin * y_state)
        moved = gathered_heads(xt * from_state)
        kept = jnp.sum(dstate * state_b.astype(f32), axis=0, keepdims=True)
        kept = kept * wide_in[SPAN - 1 : SPAN, :]
        kept = gathered_heads(jnp.broadcast_to(kept, (8, INNER)))[0:1, :]
        at_end = jnp.sum(moved, axis=0, keepdims=True) + kept
        sub = lax.broadcasted_iota(jnp.int32, (SPAN, 128), 0)
        dcum = dcum - moved + jnp.where(sub == SPAN - 1, at_end, 0.0)
        sc_state[...] = dstate * wide_in[SPAN - 1 : SPAN, :] + tn(cm, gin_b)
        inter = nt(cm, b)
        bias_m = span_bias(c, seg_ext, seg_row)
        total_t = total.T
        dinter = jnp.zeros((SPAN, SPAN), f32)
        col_sums = jnp.zeros((128, SPAN), f32)
        sub_t = lax.broadcasted_iota(jnp.int32, (128, SPAN), 0)
        ddt = jnp.zeros((SPAN, 128), f32)
        dskip = jnp.zeros((SPAN, 128), f32)
        for pair in range(HEADS // 2):
            cols = slice(128 * pair, 128 * pair + 128)
            gp, xp = grad[:, cols], xs[:, cols]
            gp_b, xp_b = gp.astype(bf16), xp.astype(bf16)
            stack = jnp.concatenate(
                [jnp.where(low2, gp, 0.0).astype(bf16), jnp.where(low2, 0.0, gp).astype(bf16)], axis=0
            )
            dm = nt(stack, xp_b)
            parts = []
            for side in range(2):
                h = 2 * pair + side
                decay = jnp.exp(total[:, h : h + 1] - total_t[h : h + 1, :] + bias_m)
                dmh = dm[side * SPAN : (side + 1) * SPAN, :] * decay
                dinter = dinter + dmh
                weight = decay * inter
                parts.append(weight.astype(bf16))
                q = dmh * inter
                dcum = dcum + jnp.where(lane == h, jnp.sum(q, axis=1, keepdims=True), 0.0)
                col_sums = col_sums + jnp.where(sub_t == h, jnp.sum(q, axis=0, keepdims=True), 0.0)
            both = tn(jnp.concatenate(parts, axis=1), gp_b)
            dxs = jnp.where(low2, both[0:SPAN, :], both[SPAN:, :]) + from_state[:, cols] * wide_tail[:, cols]
            xo = x[:, cols]
            dx = dxs * wide_dt[:, cols] + gp * skip[:, cols]
            dpre[rows, cols] = dx * slope[:, cols]
            pick_row, pick_col = head_matrix(128, 128)
            pick = jnp.where(pick_col == 2 * pair + pick_row // 64, 1.0, 0.0).astype(bf16)
            hi, lo = split_halves(dxs * xo)
            ddt = ddt + nn(hi, pick) + nn(lo, pick)
            hi, lo = split_halves(gp * xo)
            dskip = dskip + nn(hi, pick) + nn(lo, pick)
        dinter_b = dinter.astype(bf16)
        dcm = dcm + nn(dinter_b, b)
        db = db + tn(dinter_b, cm)
        dpre[rows, INNER : INNER + STATE] = db * slope[:, INNER : INNER + STATE]
        dpre[rows, INNER + STATE :] = dcm * slope[:, INNER + STATE :]
        dcum = dcum - col_sums.T
        dlog = lax.dot_general(
            tri, dcum, (((0,), (0,)), ((), ())), precision=HIGH, preferred_element_type=f32
        )
        ddt = ddt + dlog * rate[...]
        dsp = jnp.where(lane < HEADS, ddt * sigmoid(step[rows, :] + bias[...]), 0.0)
        dstep[rows, :] = dsp.astype(bf16)
        sum_decay = sum_decay + jnp.sum(dlog * own_dt, axis=0, keepdims=True)
        sum_bias = sum_bias + jnp.sum(dsp, axis=0, keepdims=True)
        sum_skip = sum_skip + jnp.sum(dskip, axis=0, keepdims=True)
    sub8 = lax.broadcasted_iota(jnp.int32, (8, 128), 0)
    heads[...] = jnp.where(
        sub8 == 0,
        sum_decay * rate[...],
        jnp.where(sub8 == 1, sum_bias, jnp.where(sub8 == 2, sum_skip, 0.0)),
    )


mixer_back = kernel_call(
    mixer_back_body,
    [((TOK, CONV), f32), ((TOK, 128), bf16), ((8, 128), f32)],
    [pltpu.VMEM((STATE, INNER), f32)],
)


def inputs_back_body(
    dpre, dpre_next, cin, taps, seg_ext, seg_next, dkv, dkv_back, cos, sin, dq, dstep, dz,
    grads, dtaps, ext,
):
    ext[0:TOK, :] = dpre[...]
    ext[TOK : TOK + 8, :] = dpre_next[...]
    run = jnp.zeros((TOK, CONV), f32)
    now = seg_next[0:TOK, 0:1]
    sub = lax.broadcasted_iota(jnp.int32, (8, CONV), 0)
    taken = jnp.zeros((8, CONV), f32)
    for k in range(4):
        ahead = 3 - k
        same = jnp.where(seg_next[ahead : ahead + TOK, 0:1] == now, 1.0, 0.0)
        run = run + ext[ahead : ahead + TOK, :] * taps[k : k + 1, :] * same
        at = HALO - 3 + k
        part = dpre[...] * cin[at : at + TOK, :] * tap_mask(seg_ext, k)
        taken = taken + jnp.where(sub == k, jnp.sum(part, axis=0, keepdims=True), 0.0)
    dtaps[...] = taken
    grads[:, C_U:] = run.astype(bf16)
    grads[:, C_Q : C_Q + QW] = dq[...]
    both = dkv[...] + dkv_back[...].astype(f32)
    low = low_half((TOK, 128))
    grads[:, C_KV : C_KV + 128] = jnp.where(low, turned(both, cos[...], -sin[...]), both).astype(bf16)
    grads[:, C_DT : C_DT + 128] = dstep[...]
    grads[:, C_Z : C_Z + INNER] = dz[...]


inputs_back = kernel_call(
    inputs_back_body,
    [((TOK, W1C), bf16), ((8, CONV), f32)],
    [pltpu.VMEM((TOK + 8, CONV), f32)],
)


def swapped(block, axis):
    return lax.ppermute(block, axis, [(0, 1), (1, 0)])


def pair_sum(block, axis):
    return block.astype(f32) + swapped(block, axis).astype(f32)


def rope_tables(positions):
    indices = jnp.arange(HEAD_WIDTH // 2).astype(f32)
    frequency = jnp.exp(indices * (-2.0 * math.log(ROPE_BASE) / HEAD_WIDTH))
    angles = positions[:, None] * frequency[None, :]
    return (jnp.tile(jnp.cos(angles), (1, 4)), jnp.tile(jnp.sin(angles), (1, 4)))


def norm_back(v, gain_row, dh):
    r = lax.rsqrt(jnp.mean(v * v, axis=1, keepdims=True) + EPS)
    scaled = dh * gain_row
    dv = r * scaled - v * (r * r * r) * jnp.mean(v * scaled, axis=1, keepdims=True)
    return dv, jnp.sum(dh * v * r, axis=0)


def lanes(vector):
    return jnp.pad(vector, (0, 128 - vector.shape[0]))[None, :]


def shards(
    tokens, segments, cotangent, gain_mixer, gain_ffn, query_proj, key_value_weight, attn_out,
    inner_proj, state_proj, step_proj, conv_inner, conv_state, decay_log, step_bias, skip_gain,
    inner_out, gate_up, down_proj,
):
    rows = query_proj.shape[0]
    ctx = lax.axis_index("ctx")
    tok = tokens.reshape(TOK, WID)
    prior = lax.ppermute(tok, "ctx", [(0, 1)])
    blocks = (
        jnp.concatenate(
            [
                query_proj,
                key_value_weight.reshape(rows, 128),
                step_proj,
                gain_mixer[:, None],
                gain_ffn[:, None],
                jnp.zeros((rows, 114), bf16),
                inner_proj.reshape(rows, 2 * INNER),
                state_proj,
            ],
            axis=1,
        ),
        jnp.concatenate([attn_out.T, inner_out.T], axis=1),
        jnp.concatenate([gate_up.reshape(rows, 2 * FFH), down_proj.T], axis=1),
    )
    w1, w2, w3 = (lax.all_gather(b, "fsdp", axis=0, tiled=True) for b in blocks)
    gains = w1[:, C_DT + HEADS : C_DT + HEADS + 2].astype(f32).T
    gain1, gain2 = gains[0:1], gains[1:2]

    start = ctx * TOK
    cos, sin = rope_tables((start + jnp.arange(TOK)).astype(f32))
    cosp, sinp = rope_tables((start - TOK + jnp.arange(TOK)).astype(f32))
    seg = segments.reshape(-1)
    late = ctx > 0
    seg_now = lax.dynamic_slice_in_dim(seg, start, TOK)
    seg_prior = jnp.where(late, seg[0:TOK], -1)
    seg_after = jnp.where(late, -2, seg[TOK : TOK + 8])
    seg_row = jnp.concatenate([seg_prior, seg_now])[None, :]
    seg_ext = jnp.concatenate([seg_prior[TOK - HALO :], seg_now])[:, None]
    seg_next = jnp.concatenate([seg_now, seg_after])[:, None]
    seg_col = seg_now[:, None]
    taps = jnp.concatenate([conv_inner, conv_state], axis=1).astype(f32)
    bias = lanes(step_bias)
    rate = lanes(-jnp.exp(decay_log))
    skip = jnp.repeat(skip_gain, 64)[None, :]

    normed, q, k2, v2, k2p, v2p, z, cin, step = project(tok, prior, w1, gain1, cos, sin, cosp, sinp)
    pre, dt, cum, last = mixer_in(cin, taps, step, bias, rate, seg_ext)
    first = lax.ppermute(last, "ctx", [(0, 1)])
    attended, lse = attend(q, k2, v2, k2p, v2p, seg_col, seg_row)
    y, gated, states = mixer_out(pre, dt, cum, seg_ext, seg_row, first, z, skip)

    mixed = jnp.concatenate([attended, gated], axis=1)
    branch = pair_sum(nt(mixed, w2).astype(bf16), "tp")
    mid = tok.astype(f32) + branch

    normed2 = (unit_rows(mid)[0] * gain2).astype(bf16)
    wgu, wdown = w3[:, 0 : 2 * FFH], w3[:, 2 * FFH :]
    gu = nn(normed2, wgu)
    gate, up = gu[:, :FFH], gu[:, FFH:]
    sig = sigmoid(gate)
    silu = gate * sig
    act = (silu * up).astype(bf16)
    cot = cotangent.reshape(TOK, WID)
    dact = nn(cot, wdown)
    dgate = dact * up * sig * (1.0 + gate * (1.0 - sig))
    dgu = jnp.concatenate([dgate, dact * silu], axis=1).astype(bf16)
    dnormed2 = pair_sum(nt(dgu, wgu).astype(bf16), "tp")
    block_out = (mid + pair_sum(nt(act, wdown).astype(bf16), "tp")).astype(bf16)
    dmid, dgain2 = norm_back(mid, gain2, dnormed2)
    grad_mid = cot.astype(f32) + dmid
    dmix = grad_mid.astype(bf16)

    w3_grad = jnp.concatenate([tn(normed2, dgu), tn(cot, act)], axis=1).astype(bf16)
    w3_part = lax.psum_scatter(w3_grad, "fsdp", scatter_dimension=0, tiled=True)

    dmixed = nn(dmix, w2)
    dattended, dgated = dmixed[:, :QW].astype(bf16), dmixed[:, QW:]
    dy, dz, dfirst = mixer_back_in(dgated, z, y, pre, cum, seg_ext)
    dlast = lax.ppermute(dfirst, "ctx", [(1, 0)])
    dq, dkv, dkv_p = attend_back(
        q, k2, v2, k2p, v2p, seg_col, seg_row, lse, dattended, cos, sin
    )
    dkv_back = lax.ppermute(dkv_p, "ctx", [(1, 0)])
    dpre, dstep, heads = mixer_back(
        dy, pre, dt, cum, seg_ext, seg_row, states, dlast, skip, rate, step, bias
    )
    dpre_next = lax.ppermute(dpre[0:8], "ctx", [(1, 0)])
    grads, dtaps = inputs_back(
        dpre, dpre_next, cin, taps, seg_ext, seg_next, dkv, dkv_back, cos, sin, dq, dstep, dz
    )
    dnormed = pair_sum(nt(grads, w1).astype(bf16), "tp")
    dtok, dgain1 = norm_back(tok.astype(f32), gain1, dnormed)
    tokens_grad = grad_mid + dtok

    w1_grad = tn(normed, grads).astype(bf16)
    w2_grad = tn(dmix, mixed).astype(bf16)
    w12_part = lax.psum_scatter(
        jnp.concatenate([w1_grad, w2_grad], axis=1), "fsdp", scatter_dimension=0, tiled=True
    )
    parts = pair_sum(jnp.concatenate([w12_part, w3_part], axis=1), "ctx")
    bc = pair_sum(parts[:, C_U + INNER : W1C].astype(bf16), "tp")

    small = jnp.concatenate([dtaps[0:4].reshape(-1), heads[0:3].reshape(-1), dgain1, dgain2])
    small = lax.psum(small, ("fsdp", "ctx"))
    taps_sum = small[0 : 4 * CONV].reshape(4, CONV)
    heads_sum = small[4 * CONV : 4 * CONV + 384].reshape(3, 128)
    gains_sum = small[4 * CONV + 384 :].reshape(2, -1, rows)
    mine = lax.dynamic_index_in_dim(gains_sum, lax.axis_index("fsdp"), 1, keepdims=False)
    state_taps = pair_sum(taps_sum[:, INNER:], "tp")

    at2, at3 = W1C, W1C + W2C
    return (
        block_out[None],
        tokens_grad[None],
        mine[0],
        mine[1],
        parts[:, 0:QW],
        parts[:, C_KV : C_KV + 128].reshape(rows, 2, 64),
        parts[:, at2 : at2 + QW].T,
        parts[:, C_Z : C_Z + 2 * INNER].reshape(rows, 2, INNER),
        bc,
        parts[:, C_DT : C_DT + HEADS],
        taps_sum[:, :INNER],
        state_taps,
        heads_sum[0, :HEADS],
        heads_sum[1, :HEADS],
        heads_sum[2, :HEADS],
        parts[:, at2 + QW : at3].T,
        parts[:, at3 : at3 + 2 * FFH].reshape(rows, 2, FFH),
        parts[:, at3 + 2 * FFH :].T,
    )


def solution(mesh):
    return jax.shard_map(
        shards,
        mesh=mesh,
        in_specs=(
            P("fsdp", "ctx", None), P("fsdp", None), P("fsdp", "ctx", None), P("fsdp"), P("fsdp"),
            P("fsdp", "tp"), P("fsdp", None, "tp"), P("tp", "fsdp"), P("fsdp", None, "tp"),
            P("fsdp", None), P("fsdp", "tp"), P(None, "tp"), P(), P("tp"), P("tp"), P("tp"),
            P("tp", "fsdp"), P("fsdp", None, "tp"), P("tp", "fsdp"),
        ),
        out_specs=(
            P("fsdp", "ctx", None), P("fsdp", "ctx", None), P("fsdp"), P("fsdp"), P("fsdp", "tp"),
            P("fsdp", None, "tp"), P("tp", "fsdp"), P("fsdp", None, "tp"), P("fsdp", None),
            P("fsdp", "tp"), P(None, "tp"), P(), P("tp"), P("tp"), P("tp"), P("tp", "fsdp"),
            P("fsdp", None, "tp"), P("tp", "fsdp"),
        ),
        check_vma=False,
    )
```

time: 1050 us -> 645 us (0.61)
  local copies, waits for them, and re-layouts: 274 us -> 32.2 us
  blocking collectives: 117 us -> 279 us
  matrix products: 189 us -> 35.4 us
  other arithmetic: 141 us -> 27 us
  Pallas kernels: 0 us -> 66.4 us
  starting transfers between devices: 84 us -> 26 us
  waiting for transfers between devices: 208 us -> 157 us
    psum x0 -> x1, blocking collectives: none -> 279 us  [shards(): small = lax.psum(small, ('fsdp', 'ctx'))]
    dot_general x96 -> x11, matrix products: 189 us -> 35.4 us  [the longest x4 14 us: tn(): lax.dot_general(a, b, (((0,), (0,)), ((), ())), preferred_element_type=f32)]
    all_to_all x19 -> x0, waiting for transfers between devices: 117 us -> none  [sent_to_all(): lax.all_to_all(jnp.broadcast_to(array[None], (devices, *array.shape)), ax...]
    dynamic_update_slice x20 -> x0, local copies, waits for them, and re-layouts: 96.2 us -> none  [ssd_scan(): lax.scan(jax.checkpoint(span_step), (state_start, seg_before), pieces)]
    all_to_all x19 -> x0, starting transfers between devices: 75.3 us -> none  [sent_to_all(): lax.all_to_all(jnp.broadcast_to(array[None], (devices, *array.shape)), ax...]
    pallas_call x0 -> x8, Pallas kernels: none -> 66.4 us  [call(): pl.pallas_call(body, out_shape=[jax.ShapeDtypeStruct(s, d) for s, d in ou...]
    unnamed x1 -> x0, blocking collectives: 63.4 us -> none
    ppermute x4 -> x12, waiting for transfers between devices: 37.3 us -> 97.6 us  [the longest x7 96 us: swapped(): return lax.ppermute(block, axis, [(0, 1), (1, 0)])]
  transfers between devices with their start and end apart: 30 -> 17, of which waited for: 18 -> 10; matrix products, arithmetic and copies ran while one was open for 41% -> 9% of each run, Pallas kernels for 0% -> 8%
where the time goes in v1:
time: 645 us; the launch traced here: 638 us
  blocking collectives  279 us (43%)
  waiting for transfers between devices  157 us (24%)
  Pallas kernels  66.4 us (10%)
  matrix products  35.4 us (5%)
  local copies, waits for them, and re-layouts  32.2 us (5%)
  other arithmetic  27 us (4%)
  starting transfers between devices  26 us (4%)
  between operations  14.5 us (2%)
    psum x1, blocking collectives, shards(): small = lax.psum(small, ('fsdp', 'ctx'))  279 us
    ppermute x7, waiting for transfers between devices, swapped(): return lax.ppermute(block, axis, [(0, 1), (1, 0)])  96 us
    pallas_call x8, Pallas kernels, call(): pl.pallas_call(body, out_shape=[jax.ShapeDtypeStruct(s, d) for s, d in ou...  66.4 us
    all_gather x3, waiting for transfers between devices, shards(): w1, w2, w3 = (lax.all_gather(b, 'fsdp', axis=0, tiled=True) for b in blocks)  59.2 us
    dot_general x4, matrix products, tn(): lax.dot_general(a, b, (((0,), (0,)), ((), ())), preferred_element_type=f32)  14 us
    ppermute x7, starting transfers between devices, swapped(): return lax.ppermute(block, axis, [(0, 1), (1, 0)])  13.9 us
    dot_general x4, matrix products, nt(): lax.dot_general(a, b, (((1,), (1,)), ((), ())), preferred_element_type=f32)  13.5 us
  transfers between devices with their start and end apart: 17, of which 10 were waited for; matrix products, arithmetic and copies ran while one was open for 9% of the time, Pallas kernels for 8%

profile of v1, /device:TPU:0, one launch (start us, length us, event | category | flops | bytes accessed | tf_op | source)
XLA Modules:
  0.0 637.8 jit_solution(13492549896431563272)
XLA Ops:
  11.2 1.5 concatenate.41
  12.8 1.4 pad_maximum_fusion.6
  15.2 1.5 pad_maximum_fusion.5
  16.8 3.5 collective-permute-start
  29.0 33.4 %all-gather.4.cloned.1.call-done.w1 = bf16[1024,2304]{1,0:T(8,128)(2,1)} async-done(((bf16[32,2304]{1,0:T(8,128)(2,1)}), bf16[1024,2304]{1,0:T(8,128)(2,1)}) %all-gather.4.cloned.1.call-update) | async-done | bytes 4718608 | tf_op jit(solution)/shard_map/all_gather | solution.py:624
  65.2 10.3 %shard_map.322 = (bf16[512,1024]{1,0:T(8,128)(2,1)}, bf16[512,256]{1,0:T(8,128)(2,1)}, bf16[512,128]{1,0:T(8,128)(2,1)}, bf16[512,128]{1,0:T(8,128)(2,1)}, bf16[...) custom-call(bf16[512,1024]{1,0:T(8,128)(2,1)} %bitcast.96, ...), custom_call_target="tpu_custom_call" | custom-call | tf_op jit(solution)/shard_map/pallas_call | solution.py:43
  75.5 6.4 %shard_map.324 = (f32[512,1024]{1,0:T(8,128)}, f32[512,128]{1,0:T(8,128)}, f32[512,128]{1,0:T(8,128)}, bf16[128,768]{1,0:T(8,128)(2,1)}) custom-call(f32[528,1024]{1,0:T(8,128)} %get-tuple-element.53.cin, f32[4,1024]{1,0:T(4,128)} %maximum_convert_fusion.taps, f32[512,128]{1,0:T(8,128)} %get-tuple-element.54.step, f32[1,128]{1,0:T(1,128)} %get-tuple-element.166.bias, ...), custom_call_target="tpu_custom_call" | custom-call | tf_op jit(solution)/shard_map/pallas_call | solution.py:43
  82.0 3.7 collective-permute-start.1
  86.2 6.0 shard_map.323
  93.9 7.3 %shard_map.325 = (f32[512,768]{1,0:T(8,128)}, bf16[512,768]{1,0:T(8,128)(2,1)}, bf16[4,128,768]{2,1,0:T(8,128)(2,1)}) custom-call(f32[512,1024]{1,0:T(8,128)} %get-tuple-element.55.pre, f32[512,128]{1,0:T(8,128)} %get-tuple-element.56.dt, f32[512,128]{1,0:T(8,128)} %get-tuple-element.57.cum, s32[528,1]{1,0:T(8,128)} %broadcast_in_dim.68.seg_ext, ...), custom_call_target="tpu_custom_call" | custom-call | tf_op jit(solution)/shard_map/pallas_call | solution.py:43
  101.2 1.2 constant_dynamic-update-slice_fusion
  102.4 6.1 all-gather.6.cloned.1.call-done
  108.5 2.9 convolution_convert_fusion.4
  111.4 3.6 collective-permute-start.2
  115.0 23.8 %collective-permute-done.2 = bf16[512,1024]{1,0:T(8,128)(2,1)S(1)} collective-permute-done((bf16[512,1024]{1,0:T(8,128)(2,1)S(1)}, bf16[512,1024]{1,0:T(8,128)(2,1)S(1)}, u32[]{:S(2)}, u32[]{:S(2)}) %collective-permute-start.2) | collective-permute-done | bytes 1048608 | tf_op jit(solution)/shard_map/ppermute | solution.py:573
  139.5 19.8 %all-gather.8.cloned.1.call-done = bf16[1024,3072]{1,0:T(8,128)(2,1)} async-done(((bf16[32,3072]{1,0:T(8,128)(2,1)}), bf16[1024,3072]{1,0:T(8,128)(2,1)}) %all-gather.8.cloned.1.call-update) | async-done | bytes 6291472 | tf_op jit(solution)/shard_map/all_gather | solution.py:624
  159.3 4.7 fusion.2
  164.1 2.0 fusion.14
  167.0 2.4 fusion.26
  169.4 3.1 collective-permute-start.4
  172.5 1.3 fusion.23
  174.6 22.4 %collective-permute-done.4 = bf16[512,1024]{1,0:T(8,128)(2,1)S(1)} collective-permute-done((bf16[512,1024]{1,0:T(8,128)(2,1)S(1)}, bf16[512,1024]{1,0:T(8,128)(2,1)S(1)}, u32[]{:S(2)}, u32[]{:S(2)}) %collective-permute-start.4) | collective-permute-done | bytes 1048608 | tf_op jit(solution)/shard_map/ppermute | solution.py:573
  197.8 21.0 %collective-permute-done.3 = bf16[512,1024]{1,0:T(8,128)(2,1)S(1)} collective-permute-done((bf16[512,1024]{1,0:T(8,128)(2,1)S(1)}, bf16[512,1024]{1,0:T(8,128)(2,1)S(1)}, u32[]{:S(2)}, u32[]{:S(2)}) %collective-permute-start.3) | collective-permute-done | bytes 1048608 | tf_op jit(solution)/shard_map/ppermute | solution.py:573
  218.8 2.0 subtract_add_fusion
  220.8 1.3 fusion.33
  222.1 1.3 slice.165.dgated
  223.4 5.9 shard_map.326
  229.3 1.3 collective-permute-start.5
  232.8 9.2 %shard_map.328 = (bf16[512,256]{1,0:T(8,128)(2,1)}, f32[512,128]{1,0:T(8,128)}, bf16[512,128]{1,0:T(8,128)(2,1)}) custom-call(bf16[512,256]{1,0:T(8,128)(2,1)} %get-tuple-element.47.q, bf16[512,128]{1,0:T(8,128)(2,1)} %get-tuple-element.48.k2, bf16[512,128]{1,0:T(8,128)(2,1)} %get-tuple-element.49.v2, bf16[512,128]{1,0:T(8,128)(2,1)} %get-tuple-element.50.k2p, ...), custom_call_target="tpu_custom_call" | custom-call | tf_op jit(solution)/shard_map/pallas_call | solution.py:43
  242.1 1.5 collective-permute-start.7
  244.3 13.2 %shard_map.327 = (f32[512,1024]{1,0:T(8,128)}, bf16[512,128]{1,0:T(8,128)(2,1)}, f32[8,128]{1,0:T(8,128)}) custom-call(f32[512,768]{1,0:T(8,128)} %get-tuple-element.62.dy, f32[512,1024]{1,0:T(8,128)} %get-tuple-element.55.pre, f32[512,128]{1,0:T(8,128)} %get-tuple-element.56.dt, f32[512,128]{1,0:T(8,128)} %get-tuple-element.57.cum, ...), custom_call_target="tpu_custom_call" | custom-call | tf_op jit(solution)/shard_map/pallas_call | solution.py:43
  258.3 1.7 collective-permute-start.6
  260.0 2.5 convolution_convert_fusion.2
  262.5 1.6 collective-permute-done.6.dpre_next
  264.7 8.0 %shard_map.329 = (bf16[512,2304]{1,0:T(8,128)(2,1)}, f32[8,1024]{1,0:T(8,128)}) custom-call(f32[512,1024]{1,0:T(8,128)} %get-tuple-element.65.dpre, f32[8,1024]{1,0:T(8,128)} %copy-done.10, f32[528,1024]{1,0:T(8,128)} %get-tuple-element.53.cin, f32[4,1024]{1,0:T(4,128)} %maximum_convert_fusion.taps, s32[528,1]{1,0:T(8,128)} %broadcast_in_dim.68.seg_ext, ...), custom_call_target="tpu_custom_call" | custom-call | tf_op jit(solution)/shard_map/pallas_call | solution.py:43
  272.7 6.0 convolution_convert_fusion
  278.7 5.6 pad_maximum_fusion
  284.5 3.0 convert_bitcast_fusion
  287.5 2.5 convolution_convert_fusion.1
  290.0 3.3 pad_maximum_fusion.1
  293.4 6.9 %convolution_convert_fusion.3 = bf16[512,1024]{1,0:T(8,128)(2,1)} fusion(bf16[512,2304]{1,0:T(8,128)(2,1)} %get-tuple-element.72, bf16[1024,2304]{1,0:T(8,128)(2,1)} %all-gather.4.cloned.1.call-done.w1), kind=kOutput, calls=%fused_computation.48 | convolution fusion | flops 2416443392 | bytes 8126464 | tf_op jit(solution)/shard_map/dot_general | solution.py:57
  300.3 3.0 collective-permute-start.8
  303.3 22.2 %collective-permute-done.8 = bf16[512,1024]{1,0:T(8,128)(2,1)} collective-permute-done((bf16[512,1024]{1,0:T(8,128)(2,1)}, bf16[512,1024]{1,0:T(8,128)(2,1)}, u32[]{:S(2)}, u32[]{:S(2)}) %collective-permute-start.8) | collective-permute-done | bytes 1048608 | tf_op jit(solution)/shard_map/ppermute | solution.py:573
  325.5 2.4 fusion.11
  328.0 279.3 %psum.7 = f32[6528]{0:T(1024)S(1)} all-reduce(f32[6528]{0:T(1024)S(1)} %pad_maximum_fusion.7), channel_id=1, replica_groups=mesh['fsdp'=32,'ctx'=2,'tp'=2] {'fsdp','ctx'}, use_global_device_ids=true, to_apply=%region_6.7 | all-reduce | flops 6528 | bytes 52224 | tf_op jit(solution)/shard_map/psum | solution.py:703
  607.3 2.8 collective-permute-start.11
  610.1 3.6 fusion.8
  618.0 5.8 collective-permute-done.9
  (147 shorter events, 38.2 us)
Async XLA Ops:
  7.2 55.2 %all-gather.4.cloned.1.call-start = ((), (), s32[]{:S(2)}) async-start(), calls=%async_computation.2 | async-start | bytes 4866048 | tf_op jit(solution)/shard_map/all_gather | solution.py:624
  12.7 95.7 %all-gather.6.cloned.1.call-start = ((), (), s32[]{:S(2)}) async-start(), calls=%async_computation.3 | async-start | bytes 2162688 | tf_op jit(solution)/shard_map/all_gather | solution.py:624
  14.3 145.1 %all-gather.8.cloned.1.call-start = ((), (), s32[]{:S(2)}) async-start(), calls=%async_computation.4 | async-start | bytes 6488064 | tf_op jit(solution)/shard_map/all_gather | solution.py:624
  16.8 9.5 %copy-start.15 = (f32[12]{0:T(128)S(1)}, f32[12]{0:T(128)}, u32[]{:S(2)}) copy-start(f32[12]{0:T(128)} %param.34) | copy-start | bytes 148
  16.8 596.9 %reduce-scatter.3.cloned.1.call-start = ((), (), s32[]{:S(2)}) async-start(), calls=%async_computation.5 | async-start | bytes 7028736 | tf_op jit(solution)/shard_map/reduce_scatter | solution.py:696
  16.8 47.4 %collective-permute-start = (bf16[512,1024]{1,0:T(8,128)(2,1)}, bf16[512,1024]{1,0:T(8,128)(2,1)S(1)}, u32[]{:S(2)}, u32[]{:S(2)}) collective-permute-start(bf16[512,1024]{1,0:T(8,128)(2,1)} %bitcast.95), channel_id=1, source_target_pairs={{0,2},{1,3},{4,6},{5,7},{8,10},{9,11},{12,14},{13,15},{16,18},{17,... | collective-permute-start | bytes 3145736 | tf_op jit(solution)/shard_map/ppermute | solution.py:606
  21.2 6.6 %copy-start.20 = (f32[12]{0:T(128)S(1)}, f32[12]{0:T(128)}, u32[]{:S(2)}) copy-start(f32[12]{0:T(128)} %param.32) | copy-start | bytes 148
  21.2 6.6 %copy-start.16 = (f32[12]{0:T(128)S(1)}, f32[12]{0:T(128)}, u32[]{:S(2)}) copy-start(f32[12]{0:T(128)} %param.33) | copy-start | bytes 148
  21.2 7.2 %copy-start.12 = (bf16[4,768]{1,0:T(4,128)(2,1)S(1)}, bf16[4,768]{1,0:T(4,128)(2,1)}, u32[]{:S(2)}) copy-start(bf16[4,768]{1,0:T(4,128)(2,1)} %param.30) | copy-start | bytes 18436
  21.2 7.2 %copy-start.13 = (bf16[4,256]{1,0:T(4,128)(2,1)S(1)}, bf16[4,256]{1,0:T(4,128)(2,1)}, u32[]{:S(2)}) copy-start(bf16[4,256]{1,0:T(4,128)(2,1)} %param.31) | copy-start | bytes 6148
  64.3 1.0 copy-start.4
  82.0 11.2 %collective-permute-start.1 = (bf16[128,768]{1,0:T(8,128)(2,1)}, bf16[128,768]{1,0:T(8,128)(2,1)S(1)}, u32[]{:S(2)}, u32[]{:S(2)}) collective-permute-start(bf16[128,768]{1,0:T(8,128)(2,1)} %get-tuple-element.58), channel_id=1, source_target_pairs={{0,2},{1,3},{4,6},{5,7},{8,10},{9,11},{12,14},{13,15},{16,18},{17,... | collective-permute-start | bytes 589832 | tf_op jit(solution)/shard_map/ppermute | solution.py:647
  93.2 0.7 copy-start.6
  102.4 9.0 %copy-start.9 = (bf16[512,1024]{1,0:T(8,128)(2,1)}, bf16[512,1024]{1,0:T(8,128)(2,1)S(1)}, u32[]{:S(2)}) copy-start(bf16[512,1024]{1,0:T(8,128)(2,1)S(1)} %constant_dynamic-update-slice_fusion) | copy-start | bytes 3145732
  102.4 36.4 %copy-start = (bf16[1,512,1024]{2,1,0:T(8,128)(2,1)S(1)}, bf16[1,512,1024]{2,1,0:T(8,128)(2,1)}, u32[]{:S(2)}) copy-start(bf16[1,512,1024]{2,1,0:T(8,128)(2,1)} %param.19) | copy-start | bytes 3145732
  111.4 27.4 %collective-permute-start.2 = (bf16[512,1024]{1,0:T(8,128)(2,1)S(1)}, bf16[512,1024]{1,0:T(8,128)(2,1)S(1)}, u32[]{:S(2)}, u32[]{:S(2)}) collective-permute-start(bf16[512,1024]{1,0:T(8,128)(2,1)S(1)} %convolution_convert_fusion.4), channel_id=1, source_target_pairs={{0,1},{1,0},{2,3},{3,2},{4,5},{5,4},{6,7},{7,6},{8,9},{9,8},{10,11... | collective-permute-start | bytes 3145736 | tf_op jit(solution)/shard_map/ppermute | solution.py:573
  159.3 4.7 copy-start.3
  159.3 4.7 copy-start.17
  166.0 1.0 copy-start.22
  166.1 3.3 copy-start.24
  166.1 6.4 %copy-start.21 = (bf16[512,1024]{1,0:T(8,128)(2,1)}, bf16[512,1024]{1,0:T(8,128)(2,1)S(1)}, u32[]{:S(2)}) copy-start(bf16[512,1024]{1,0:T(8,128)(2,1)S(1)} %get-tuple-element.138) | copy-start | bytes 3145732
  169.4 27.6 %collective-permute-start.4 = (bf16[512,1024]{1,0:T(8,128)(2,1)S(1)}, bf16[512,1024]{1,0:T(8,128)(2,1)S(1)}, u32[]{:S(2)}, u32[]{:S(2)}) collective-permute-start(bf16[512,1024]{1,0:T(8,128)(2,1)S(1)} %fusion.26), channel_id=1, source_target_pairs={{0,1},{1,0},{2,3},{3,2},{4,5},{5,4},{6,7},{7,6},{8,9},{9,8},{10,11... | collective-permute-start | bytes 3145736 | tf_op jit(solution)/shard_map/ppermute | solution.py:573
  173.8 45.0 %collective-permute-start.3 = (bf16[512,1024]{1,0:T(8,128)(2,1)S(1)}, bf16[512,1024]{1,0:T(8,128)(2,1)S(1)}, u32[]{:S(2)}, u32[]{:S(2)}) collective-permute-start(bf16[512,1024]{1,0:T(8,128)(2,1)S(1)} %fusion.23), channel_id=1, source_target_pairs={{0,1},{1,0},{2,3},{3,2},{4,5},{5,4},{6,7},{7,6},{8,9},{9,8},{10,11... | collective-permute-start | bytes 3145736 | tf_op jit(solution)/shard_map/ppermute | solution.py:573
  218.8 2.0 copy-start.18
  220.8 39.2 %copy-start.1 = (f32[512,1024]{1,0:T(8,128)}, f32[512,1024]{1,0:T(8,128)S(1)}, u32[]{:S(2)}) copy-start(f32[512,1024]{1,0:T(8,128)S(1)} %get-tuple-element.139) | copy-start | bytes 6291460
  229.3 14.3 %collective-permute-start.5 = (bf16[128,768]{1,0:T(8,128)(2,1)}, bf16[128,768]{1,0:T(8,128)(2,1)S(1)}, u32[]{:S(2)}, u32[]{:S(2)}) collective-permute-start(bf16[128,768]{1,0:T(8,128)(2,1)} %get-tuple-element.64), channel_id=1, source_target_pairs={{2,0},{3,1},{6,4},{7,5},{10,8},{11,9},{14,12},{15,13},{18,16},{19,... | collective-permute-start | bytes 589832 | tf_op jit(solution)/shard_map/ppermute | solution.py:678
  242.1 20.4 %collective-permute-start.7 = (bf16[512,128]{1,0:T(8,128)(2,1)}, bf16[512,128]{1,0:T(8,128)(2,1)S(1)}, u32[]{:S(2)}, u32[]{:S(2)}) collective-permute-start(bf16[512,128]{1,0:T(8,128)(2,1)} %get-tuple-element.68), channel_id=1, source_target_pairs={{2,0},{3,1},{6,4},{7,5},{10,8},{11,9},{14,12},{15,13},{18,16},{19,... | collective-permute-start | bytes 393224 | tf_op jit(solution)/shard_map/ppermute | solution.py:682
  243.6 0.7 copy-start.5
  258.3 5.8 collective-permute-start.6
  262.5 1.6 copy-start.7
  264.1 0.6 copy-start.10
  264.7 8.0 %copy-start.19 = (bf16[512,1024]{1,0:T(8,128)(2,1)S(1)}, bf16[512,1024]{1,0:T(8,128)(2,1)}, u32[]{:S(2)}) copy-start(bf16[512,1024]{1,0:T(8,128)(2,1)} %get-tuple-element.75) | copy-start | bytes 3145732
  284.3 330.3 %reduce-scatter.5.cloned.1.call-start = ((), (), s32[]{:S(2)}) async-start(), calls=%async_computation.6 | async-start | bytes 6488064 | tf_op jit(solution)/shard_map/reduce_scatter | solution.py:673
  284.5 3.0 copy-start.23
  284.5 3.0 copy-start.25
  293.3 10.0 %copy-start.14 = (f32[8,128]{1,0:T(8,128)S(1)}, f32[8,128]{1,0:T(8,128)}, u32[]{:S(2)}) copy-start(f32[8,128]{1,0:T(8,128)} %get-tuple-element.74) | copy-start | bytes 12292
  293.4 10.0 %copy-start.11 = (f32[8,1024]{1,0:T(8,128)S(1)}, f32[8,1024]{1,0:T(8,128)}, u32[]{:S(2)}) copy-start(f32[8,1024]{1,0:T(8,128)} %get-tuple-element.73) | copy-start | bytes 98308
  293.4 32.1 %copy-start.8 = (f32[1,1024]{1,0:T(1,128)S(1)}, f32[1,1024]{1,0:T(1,128)}, u32[]{:S(2)}) copy-start(f32[1,1024]{1,0:T(1,128)} %get-tuple-element.147.gain) | copy-start | bytes 12292
  300.3 309.8 %copy-start.2 = (f32[512,1024]{1,0:T(8,128)S(1)}, f32[512,1024]{1,0:T(8,128)}, u32[]{:S(2)}) copy-start(f32[512,1024]{1,0:T(8,128)} %copy-done.1) | copy-start | bytes 6291460
  300.3 25.2 %collective-permute-start.8 = (bf16[512,1024]{1,0:T(8,128)(2,1)}, bf16[512,1024]{1,0:T(8,128)(2,1)}, u32[]{:S(2)}, u32[]{:S(2)}) collective-permute-start(bf16[512,1024]{1,0:T(8,128)(2,1)} %convolution_convert_fusion.3), channel_id=1, source_target_pairs={{0,1},{1,0},{2,3},{3,2},{4,5},{5,4},{6,7},{7,6},{8,9},{9,8},{10,11... | collective-permute-start | bytes 3145736 | tf_op jit(solution)/shard_map/ppermute | solution.py:573
  607.3 10.1 %collective-permute-start.11 = (f32[4,256]{1,0:T(4,128)S(1)}, f32[4,256]{1,0:T(4,128)S(1)}, u32[]{:S(2)}, u32[]{:S(2)}) collective-permute-start(f32[4,256]{1,0:T(4,128)S(1)} %slice.176), channel_id=1, source_target_pairs={{0,1},{1,0},{2,3},{3,2},{4,5},{5,4},{6,7},{7,6},{8,9},{9,8},{10,11... | collective-permute-start | bytes 12296 | tf_op jit(solution)/shard_map/ppermute | solution.py:573
  615.6 8.2 %collective-permute-start.9 = (bf16[32,6400]{1,0:T(8,128)(2,1)S(1)}, bf16[32,6400]{1,0:T(8,128)(2,1)S(1)}, u32[]{:S(2)}, u32[]{:S(2)}) collective-permute-start(bf16[32,6400]{1,0:T(8,128)(2,1)S(1)} %constant_dynamic-update-slice_fusion.2), channel_id=1, source_target_pairs={{0,2},{2,0},{1,3},{3,1},{4,6},{6,4},{5,7},{7,5},{8,10},{10,8},{9,1... | collective-permute-start | bytes 1228808 | tf_op jit(solution)/shard_map/ppermute | solution.py:573
  625.2 5.2 collective-permute-start.10
Sparse Core Ops, SparseCore 0:
  12.9 49.4 all-gather.3
  65.2 43.2 all-gather.5
  110.7 48.5 all-gather.7
  284.4 86.0 reduce-scatter.2
  374.6 85.6 reduce-scatter.4

commit v2 on v1

--- a/solution.py
+++ b/solution.py
@@ -569,6 +569,299 @@
 )
 
 
+MESH = pl.DeviceIdType.MESH
+GC = W1C + W2C
+PIECE = 256
+PIECES = GC // PIECE
+A_PIECES = 7
+COLS = (slice(0, A_PIECES * PIECE), slice(A_PIECES * PIECE, GC))
+BC0 = C_U + INNER
+SHARE = 384
+SMALL = CONV + 128
+
+
+def place():
+    f = lax.axis_index("fsdp")
+    core = lax.rem(f, 2)
+    chip = lax.div(f, 2)
+    return lax.div(chip, 4), lax.rem(chip, 4), core
+
+
+def at_yz(y, z, core):
+    return {"fsdp": (lax.rem(y, 4) * 4 + lax.rem(z, 4)) * 2 + core}
+
+
+def greet(peers):
+    barrier = pltpu.get_barrier_semaphore()
+    for peer in peers:
+        pl.semaphore_signal(barrier, inc=1, device_id=peer, device_id_type=MESH)
+    pl.semaphore_wait(barrier, len(peers))
+
+
+def send(src, dst, sems, k, peer):
+    copy = pltpu.make_async_remote_copy(
+        src_ref=src,
+        dst_ref=dst,
+        send_sem=sems.at[0, k],
+        recv_sem=sems.at[1, k],
+        device_id=peer,
+        device_id_type=MESH,
+    )
+    copy.start()
+    return copy
+
+
+class RingSum:
+    def __init__(self, chunk, me, right, left, sems, far, near, joined):
+        self.chunk, self.me, self.sems = chunk, me, sems
+        self.right, self.left = right, left
+        self.far, self.near, self.joined = far, near, joined
+        self.sent = []
+
+    def ahead(self, n):
+        return lax.rem(self.me + n, 4)
+
+    def start(self):
+        c, s = self.chunk, self.sems
+        self.far_copies = (
+            send(c(self.ahead(2), 0), self.far.at[0], s, 0, self.right),
+            send(c(self.ahead(2), 1), self.far.at[1], s, 1, self.left),
+        )
+        self.direct = (
+            send(c(self.ahead(1), 1), self.near.at[0, 1], s, 2, self.right),
+            send(c(self.ahead(3), 0), self.near.at[1, 0], s, 3, self.left),
+        )
+
+    def forward(self):
+        c, s = self.chunk, self.sems
+        passed = []
+        for side, (peer, n) in enumerate(((self.right, 1), (self.left, 3))):
+            self.far_copies[side].wait_recv()
+            own = c(self.ahead(n), side)[...]
+            self.joined[side] = (own.astype(f32) + self.far[side].astype(f32)).astype(bf16)
+            passed.append(send(self.joined.at[side], self.near.at[side, side], s, 4 + side, peer))
+        self.passed = tuple(passed)
+
+    def finish(self):
+        for copy in self.direct + self.passed:
+            copy.wait_recv()
+
+    def total(self, half):
+        own = self.chunk(self.me, half)[...].astype(f32)
+        return own + self.near[0, half].astype(f32) + self.near[1, half].astype(f32)
+
+    def close(self):
+        for copy in self.far_copies + self.direct + self.passed:
+            copy.wait_send()
+
+
+def tail_body(
+    normed, grads, dmix, mixed, w1, tok, gain, gmid, dgain2, small,
+    parts, tok_grad, small_out,
+    dn, dn_back, gbuf, crecv, acc, far_a, near_a, join_a, far_b, near_b, join_b, one_a, one_b,
+    far_a2, near_a2, join_a2, far_b2, near_b2, join_b2, fin, fin_back, share, share_back,
+    sm_core, sm_z, sm_y, sm_ctx, sm_tp,
+    tp_sems, core_sems, a_sems, b_sems, a2_sems, b2_sems, ctx_sems, small_sems,
+):
+    y, z, core = place()
+    ctx, tp = lax.axis_index("ctx"), lax.axis_index("tp")
+    sibling = at_yz(y, z, 1 - core)
+    z_peers = [at_yz(y, z + n, core) for n in (1, 2, 3)]
+    y_peers = [at_yz(y + n, z, core) for n in (1, 2, 3)]
+    ctx_peer, tp_peer = {"ctx": 1 - ctx}, {"tp": 1 - tp}
+    greet([sibling, ctx_peer, tp_peer] + z_peers + y_peers)
+
+    sm_core[core] = small[...]
+    small_copies = [send(sm_core.at[core], sm_core.at[core], small_sems, 0, sibling)]
+
+    @pl.loop(0, WID // 256)
+    def _(j):
+        to = pl.ds(pl.multiple_of(j * 256, 256), 256)
+        dn[:, to] = nt(grads[...], w1[to, :]).astype(bf16)
+
+    dn_copy = send(dn, dn_back, tp_sems, 0, tp_peer)
+    v = tok[...].astype(f32)
+    dgain1 = jnp.sum(dn[...].astype(f32) * unit_rows(v)[0], axis=0, keepdims=True)
+    sub = lax.broadcasted_iota(jnp.int32, (128, WID), 0)
+    gain_rows = jnp.where(sub == HEADS, dgain1, jnp.where(sub == HEADS + 1, dgain2[...] * 0.5, 0.0))
+
+    core_copies = []
+
+    def piece(j):
+        cols = slice(j * PIECE, (j + 1) * PIECE)
+        if j < W1C // PIECE:
+            block = tn(normed[...], grads[:, cols])
+        else:
+            at = slice(j * PIECE - W1C, (j + 1) * PIECE - W1C)
+            block = tn(dmix[...], mixed[:, at])
+        if j == C_DT // PIECE:
+            block = jnp.concatenate([block[:, 0:128], block[:, 128:256] + gain_rows.T], axis=1)
+        gbuf[:, :, :, :, cols] = block.astype(bf16).reshape(4, 4, 2, 32, PIECE)
+        core_copies.append(
+            send(
+                gbuf.at[:, :, 1 - core, :, cols], crecv.at[:, :, :, cols], core_sems, j, sibling
+            )
+        )
+
+    def add_piece(j):
+        cols = slice(j * PIECE, (j + 1) * PIECE)
+        core_copies[j].wait_recv()
+        own = gbuf[:, :, core, :, cols]
+        acc[:, :, :, cols] = (own.astype(f32) + crecv[:, :, :, cols].astype(f32)).astype(bf16)
+
+    ca, cb = COLS
+    ring_a = RingSum(
+        lambda d, h: acc.at[2 * h : 2 * h + 2, d, :, ca], z, z_peers[0], z_peers[2], a_sems,
+        far_a, near_a, join_a,
+    )
+    ring_b = RingSum(
+        lambda d, h: acc.at[d, 2 * h : 2 * h + 2, :, cb], y, y_peers[0], y_peers[2], b_sems,
+        far_b, near_b, join_b,
+    )
+    ring_a2 = RingSum(
+        lambda d, h: one_a.at[d, 16 * h : 16 * h + 16, :], y, y_peers[0], y_peers[2], a2_sems,
+        far_a2, near_a2, join_a2,
+    )
+    ring_b2 = RingSum(
+        lambda d, h: one_b.at[d, 16 * h : 16 * h + 16, :], z, z_peers[0], z_peers[2], b2_sems,
+        far_b2, near_b2, join_b2,
+    )
+
+    for j in range(PIECES + 1):
+        if j < PIECES:
+            piece(j)
+        if j > 0:
+            add_piece(j - 1)
+        if j == A_PIECES:
+            ring_a.start()
+            small_copies[0].wait_recv()
+            sm_z[z] = sm_core[0] + sm_core[1]
+            z_copies = [
+                send(sm_z.at[z], sm_z.at[z], small_sems, 1 + n, peer)
+                for n, peer in enumerate(z_peers)
+            ]
+            small_copies += z_copies
+    ring_b.start()
+    ring_a.forward()
+    ring_b.forward()
+    ring_a.finish()
+    for h in range(2):
+        one_a[2 * h : 2 * h + 2] = ring_a.total(h).astype(bf16)
+    ring_a2.start()
+    for copy in z_copies:
+        copy.wait_recv()
+    sm_y[y] = (sm_z[0] + sm_z[1]) + (sm_z[2] + sm_z[3])
+    y_copies = [
+        send(sm_y.at[y], sm_y.at[y], small_sems, 4 + n, peer) for n, peer in enumerate(y_peers)
+    ]
+    small_copies += y_copies
+    ring_b.finish()
+    for h in range(2):
+        one_b[2 * h : 2 * h + 2] = ring_b.total(h).astype(bf16)
+    ring_b2.start()
+    ring_a2.forward()
+    ring_b2.forward()
+    ring_a2.finish()
+    for h in range(2):
+        fin[16 * h : 16 * h + 16, ca] = ring_a2.total(h).astype(bf16)
+    ring_b2.finish()
+    for h in range(2):
+        fin[16 * h : 16 * h + 16, cb] = ring_b2.total(h).astype(bf16)
+    fin_copy = send(fin, fin_back, ctx_sems, 0, ctx_peer)
+    for copy in y_copies:
+        copy.wait_recv()
+    sm_ctx[ctx] = (sm_y[0] + sm_y[1]) + (sm_y[2] + sm_y[3])
+    ctx_copy = send(sm_ctx.at[ctx], sm_ctx.at[ctx], small_sems, 7, ctx_peer)
+
+    dn_copy.wait_recv()
+    dh = (dn[...].astype(f32) + dn_back[...].astype(f32)) * gain[...]
+    r = lax.rsqrt(jnp.mean(v * v, axis=1, keepdims=True) + EPS)
+    inner = jnp.mean(v * dh, axis=1, keepdims=True)
+    tok_grad[...] = gmid[...] + r * dh - v * (r * r * r * inner)
+
+    fin_copy.wait_recv()
+    total = fin[...].astype(f32) + fin_back[...].astype(f32)
+    parts[...] = total
+    share[:, 0:128] = total[:, C_DT : C_DT + 128].astype(bf16)
+    share[:, 128:384] = total[:, BC0 : BC0 + 256].astype(bf16)
+    share_copy = send(share, share_back, ctx_sems, 1, tp_peer)
+    ctx_copy.wait_recv()
+    sums = sm_ctx[0] + sm_ctx[1]
+    small_out[...] = sums
+    sm_tp[tp] = sums[0:4, INNER:CONV]
+    last_copy = send(sm_tp.at[tp], sm_tp.at[tp], small_sems, 8, tp_peer)
+    share_copy.wait_recv()
+    both = share[...].astype(f32) + share_back[...].astype(f32)
+    lane = lax.broadcasted_iota(jnp.int32, (32, 128), 1)
+    parts[:, C_DT : C_DT + 128] = jnp.where(lane < HEADS, total[:, C_DT : C_DT + 128], both[:, 0:128])
+    parts[:, BC0 : BC0 + 256] = both[:, 128:384]
+    last_copy.wait_recv()
+    small_out[0:4, INNER:CONV] = sm_tp[0] + sm_tp[1]
+
+    for ring in (ring_a, ring_b, ring_a2, ring_b2):
+        ring.close()
+    for copy in core_copies + small_copies + [dn_copy, fin_copy, ctx_copy, share_copy, last_copy]:
+        copy.wait_send()
+
+
+def tail(*args):
+    wide_a, wide_b = A_PIECES * PIECE, GC - A_PIECES * PIECE
+
+    def ring_space(lead, wide):
+        return [
+            pltpu.VMEM((2,) + lead + (wide,), bf16),
+            pltpu.VMEM((2, 2) + lead + (wide,), bf16),
+            pltpu.VMEM((2,) + lead + (wide,), bf16),
+        ]
+
+    def sems(n):
+        return pltpu.SemaphoreType.DMA((2, n))
+
+    return pl.pallas_call(
+        tail_body,
+        out_shape=[
+            jax.ShapeDtypeStruct((32, GC), f32),
+            jax.ShapeDtypeStruct((TOK, WID), f32),
+            jax.ShapeDtypeStruct((8, SMALL), f32),
+        ],
+        in_specs=vmem(len(args)),
+        out_specs=vmem(3),
+        scratch_shapes=[
+            pltpu.VMEM((TOK, WID), bf16),
+            pltpu.VMEM((TOK, WID), bf16),
+            pltpu.VMEM((4, 4, 2, 32, GC), bf16),
+            pltpu.VMEM((4, 4, 32, GC), bf16),
+            pltpu.VMEM((4, 4, 32, GC), bf16),
+            *ring_space((2, 32), wide_a),
+            *ring_space((2, 32), wide_b),
+            pltpu.VMEM((4, 32, wide_a), bf16),
+            pltpu.VMEM((4, 32, wide_b), bf16),
+            *ring_space((16,), wide_a),
+            *ring_space((16,), wide_b),
+            pltpu.VMEM((32, GC), bf16),
+            pltpu.VMEM((32, GC), bf16),
+            pltpu.VMEM((32, SHARE), bf16),
+            pltpu.VMEM((32, SHARE), bf16),
+            pltpu.VMEM((2, 8, SMALL), f32),
+            pltpu.VMEM((4, 8, SMALL), f32),
+            pltpu.VMEM((4, 8, SMALL), f32),
+            pltpu.VMEM((2, 8, SMALL), f32),
+            pltpu.VMEM((2, 4, CONV - INNER), f32),
+            sems(1),
+            sems(PIECES),
+            sems(6),
+            sems(6),
+            sems(6),
+            sems(6),
+            sems(2),
+            sems(9),
+        ],
+        compiler_params=pltpu.CompilerParams(
+            vmem_limit_bytes=60 * 1024 * 1024, collective_id=0, has_side_effects=True
+        ),
+    )(*args)
+
+
 def swapped(block, axis):
     return lax.ppermute(block, axis, [(0, 1), (1, 0)])
 
@@ -664,7 +957,8 @@
     dgate = dact * up * sig * (1.0 + gate * (1.0 - sig))
     dgu = jnp.concatenate([dgate, dact * silu], axis=1).astype(bf16)
     dnormed2 = pair_sum(nt(dgu, wgu).astype(bf16), "tp")
-    block_out = (mid + pair_sum(nt(act, wdown).astype(bf16), "tp")).astype(bf16)
+    down, dnormed2 = lax.optimization_barrier((nt(act, wdown).astype(bf16), dnormed2))
+    block_out = (mid + pair_sum(down, "tp")).astype(bf16)
     dmid, dgain2 = norm_back(mid, gain2, dnormed2)
     grad_mid = cot.astype(f32) + dmid
     dmix = grad_mid.astype(bf16)
@@ -687,46 +981,33 @@
     grads, dtaps = inputs_back(
         dpre, dpre_next, cin, taps, seg_ext, seg_next, dkv, dkv_back, cos, sin, dq, dstep, dz
     )
-    dnormed = pair_sum(nt(grads, w1).astype(bf16), "tp")
-    dtok, dgain1 = norm_back(tok.astype(f32), gain1, dnormed)
-    tokens_grad = grad_mid + dtok
-
-    w1_grad = tn(normed, grads).astype(bf16)
-    w2_grad = tn(dmix, mixed).astype(bf16)
-    w12_part = lax.psum_scatter(
-        jnp.concatenate([w1_grad, w2_grad], axis=1), "fsdp", scatter_dimension=0, tiled=True
-    )
-    parts = pair_sum(jnp.concatenate([w12_part, w3_part], axis=1), "ctx")
-    bc = pair_sum(parts[:, C_U + INNER : W1C].astype(bf16), "tp")
-
-    small = jnp.concatenate([dtaps[0:4].reshape(-1), heads[0:3].reshape(-1), dgain1, dgain2])
-    small = lax.psum(small, ("fsdp", "ctx"))
-    taps_sum = small[0 : 4 * CONV].reshape(4, CONV)
-    heads_sum = small[4 * CONV : 4 * CONV + 384].reshape(3, 128)
-    gains_sum = small[4 * CONV + 384 :].reshape(2, -1, rows)
-    mine = lax.dynamic_index_in_dim(gains_sum, lax.axis_index("fsdp"), 1, keepdims=False)
-    state_taps = pair_sum(taps_sum[:, INNER:], "tp")
-
-    at2, at3 = W1C, W1C + W2C
+    small = jnp.concatenate([dtaps, heads], axis=1)
+    parts, tokens_grad, sums = tail(
+        normed, grads, dmix, mixed, w1, tok, gain1, grad_mid, dgain2[None, :], small
+    )
+    parts3 = pair_sum(w3_part, "ctx")
+    mine = parts[:, C_DT + HEADS : C_DT + HEADS + 2]
+
+    at2 = W1C
     return (
         block_out[None],
         tokens_grad[None],
-        mine[0],
-        mine[1],
+        mine[:, 0],
+        mine[:, 1],
         parts[:, 0:QW],
         parts[:, C_KV : C_KV + 128].reshape(rows, 2, 64),
         parts[:, at2 : at2 + QW].T,
         parts[:, C_Z : C_Z + 2 * INNER].reshape(rows, 2, INNER),
-        bc,
+        parts[:, BC0 : BC0 + 256],
         parts[:, C_DT : C_DT + HEADS],
-        taps_sum[:, :INNER],
-        state_taps,
-        heads_sum[0, :HEADS],
-        heads_sum[1, :HEADS],
-        heads_sum[2, :HEADS],
-        parts[:, at2 + QW : at3].T,
-        parts[:, at3 : at3 + 2 * FFH].reshape(rows, 2, FFH),
-        parts[:, at3 + 2 * FFH :].T,
+        sums[0:4, :INNER],
+        sums[0:4, INNER:CONV],
+        sums[0, CONV : CONV + HEADS],
+        sums[1, CONV : CONV + HEADS],
+        sums[2, CONV : CONV + HEADS],
+        parts[:, at2 + QW :].T,
+        parts3[:, : 2 * FFH].reshape(rows, 2, FFH),
+        parts3[:, 2 * FFH :].T,
     )
 
 

time: 645 us -> 384 us (0.60)
  blocking collectives: 279 us -> 0 us
  Pallas kernels: 66.4 us -> 126 us
  waiting for transfers between devices: 157 us -> 134 us
  matrix products: 35.4 us -> 24.3 us
  other arithmetic: 27 us -> 17.5 us
    psum x1 -> x0, blocking collectives: 279 us -> none  [shards(): small = lax.psum(small, ('fsdp', 'ctx'))]
    pallas_call x0 -> x1, Pallas kernels: none -> 59.4 us  [tail(): pl.pallas_call(tail_body, out_shape=[jax.ShapeDtypeStruct((32, GC), f32),...]
    ppermute x7 -> x4, waiting for transfers between devices: 96 us -> 70 us  [swapped(): return lax.ppermute(block, axis, [(0, 1), (1, 0)])]
    dot_general x4 -> x2, matrix products: 14 us -> 3.82 us  [tn(): lax.dot_general(a, b, (((0,), (0,)), ((), ())), preferred_element_type=f32)]
    ppermute x7 -> x4, starting transfers between devices: 13.9 us -> 10.7 us  [swapped(): return lax.ppermute(block, axis, [(0, 1), (1, 0)])]
    dot_general x4 -> x3, matrix products: 13.5 us -> 11 us  [nt(): lax.dot_general(a, b, (((1,), (1,)), ((), ())), preferred_element_type=f32)]
  transfers between devices with their start and end apart: 17 -> 13, of which waited for: 10 -> 8; matrix products, arithmetic and copies ran while one was open for 9% -> 14% of each run, Pallas kernels for 8% -> 33%
where the time goes in v2:
time: 384 us; the launch traced here: 377 us
  waiting for transfers between devices  134 us (35%)
  Pallas kernels  126 us (33%)
  local copies, waits for them, and re-layouts  38.5 us (10%)
  matrix products  24.3 us (6%)
  starting transfers between devices  22.6 us (6%)
  other arithmetic  17.5 us (5%)
  between operations  14.4 us (4%)
    ppermute x4, waiting for transfers between devices, swapped(): return lax.ppermute(block, axis, [(0, 1), (1, 0)])  70 us
    pallas_call x8, Pallas kernels, call(): pl.pallas_call(body, out_shape=[jax.ShapeDtypeStruct(s, d) for s, d in ou...  66.5 us
    all_gather x3, waiting for transfers between devices, shards(): w1, w2, w3 = (lax.all_gather(b, 'fsdp', axis=0, tiled=True) for b in blocks)  60.1 us
    pallas_call x1, Pallas kernels, tail(): pl.pallas_call(tail_body, out_shape=[jax.ShapeDtypeStruct((32, GC), f32),...  59.4 us
    dot_general x3, matrix products, nt(): lax.dot_general(a, b, (((1,), (1,)), ((), ())), preferred_element_type=f32)  11 us
    ppermute x4, starting transfers between devices, swapped(): return lax.ppermute(block, axis, [(0, 1), (1, 0)])  10.7 us
    dot_general x3, matrix products, nn(): return jnp.dot(a, b, preferred_element_type=f32)  9.46 us
    unnamed x47, local copies, waits for them, and re-layouts  8.76 us
  transfers between devices with their start and end apart: 13, of which 8 were waited for; matrix products, arithmetic and copies ran while one was open for 14% of the time, Pallas kernels for 33%

profile of v2, /device:TPU:0, one launch (start us, length us, event | category | flops | bytes accessed | tf_op | source)
XLA Modules:
  0.0 377.0 jit_solution(12516643557656131368)
XLA Ops:
  11.2 1.5 concatenate.35
  12.8 1.4 pad_maximum_fusion.5
  15.2 1.5 pad_maximum_fusion.4
  16.9 3.5 collective-permute-start
  29.0 33.4 %all-gather.4.cloned.1.call-done.w1 = bf16[1024,2304]{1,0:T(8,128)(2,1)} async-done(((bf16[32,2304]{1,0:T(8,128)(2,1)}), bf16[1024,2304]{1,0:T(8,128)(2,1)}) %all-gather.4.cloned.1.call-update) | async-done | bytes 4718608 | tf_op jit(solution)/shard_map/all_gather | solution.py:917
  65.2 10.3 %shard_map.322 = (bf16[512,1024]{1,0:T(8,128)(2,1)}, bf16[512,256]{1,0:T(8,128)(2,1)}, bf16[512,128]{1,0:T(8,128)(2,1)}, bf16[512,128]{1,0:T(8,128)(2,1)}, bf16[...) custom-call(bf16[512,1024]{1,0:T(8,128)(2,1)} %bitcast.75, ...), custom_call_target="tpu_custom_call" | custom-call | tf_op jit(solution)/shard_map/pallas_call | solution.py:43
  75.6 6.4 %shard_map.324 = (f32[512,1024]{1,0:T(8,128)}, f32[512,128]{1,0:T(8,128)}, f32[512,128]{1,0:T(8,128)}, bf16[128,768]{1,0:T(8,128)(2,1)}) custom-call(f32[528,1024]{1,0:T(8,128)} %get-tuple-element.58.cin, f32[4,1024]{1,0:T(4,128)} %maximum_convert_fusion.taps, f32[512,128]{1,0:T(8,128)} %get-tuple-element.59.step, f32[1,128]{1,0:T(1,128)} %get-tuple-element.173.bias, ...), custom_call_target="tpu_custom_call" | custom-call | tf_op jit(solution)/shard_map/pallas_call | solution.py:43
  82.0 3.8 %collective-permute-start.1 = (bf16[128,768]{1,0:T(8,128)(2,1)}, bf16[128,768]{1,0:T(8,128)(2,1)S(1)}, u32[]{:S(2)}, u32[]{:S(2)}) collective-permute-start(bf16[128,768]{1,0:T(8,128)(2,1)} %get-tuple-element.63), channel_id=1, source_target_pairs={{0,2},{1,3},{4,6},{5,7},{8,10},{9,11},{12,14},{13,15},{16,18},{17,... | collective-permute-start | bytes 589832 | tf_op jit(solution)/shard_map/ppermute | solution.py:940
  86.4 6.0 %shard_map.323 = (bf16[512,256]{1,0:T(8,128)(2,1)}, f32[512,128]{1,0:T(8,128)}) custom-call(bf16[512,256]{1,0:T(8,128)(2,1)} %get-tuple-element.52.q, bf16[512,128]{1,0:T(8,128)(2,1)} %get-tuple-element.53.k2, bf16[512,128]{1,0:T(8,128)(2,1)} %get-tuple-element.54.v2, bf16[512,128]{1,0:T(8,128)(2,1)} %get-tuple-element.55.k2p, ...), custom_call_target="tpu_custom_call" | custom-call | tf_op jit(solution)/shard_map/pallas_call | solution.py:43
  94.1 7.3 %shard_map.325 = (f32[512,768]{1,0:T(8,128)}, bf16[512,768]{1,0:T(8,128)(2,1)}, bf16[4,128,768]{2,1,0:T(8,128)(2,1)}) custom-call(f32[512,1024]{1,0:T(8,128)} %get-tuple-element.60.pre, f32[512,128]{1,0:T(8,128)} %get-tuple-element.61.dt, f32[512,128]{1,0:T(8,128)} %get-tuple-element.62.cum, s32[528,1]{1,0:T(8,128)} %broadcast_in_dim.70.seg_ext, ...), custom_call_target="tpu_custom_call" | custom-call | tf_op jit(solution)/shard_map/pallas_call | solution.py:43
  101.4 1.2 constant_dynamic-update-slice_fusion.mixed
  102.6 5.8 %all-gather.6.cloned.1.call-done = bf16[1024,1024]{1,0:T(8,128)(2,1)} async-done(((bf16[32,1024]{1,0:T(8,128)(2,1)}), bf16[1024,1024]{1,0:T(8,128)(2,1)}) %all-gather.6.cloned.1.call-update) | async-done | bytes 2097168 | tf_op jit(solution)/shard_map/all_gather | solution.py:917
  108.5 2.9 convolution_convert_fusion.1
  111.4 3.2 collective-permute-start.2
  114.6 23.8 %collective-permute-done.2 = bf16[512,1024]{1,0:T(8,128)(2,1)S(1)} collective-permute-done((bf16[512,1024]{1,0:T(8,128)(2,1)S(1)}, bf16[512,1024]{1,0:T(8,128)(2,1)S(1)}, u32[]{:S(2)}, u32[]{:S(2)}) %collective-permute-start.2) | collective-permute-done | bytes 1048608 | tf_op jit(solution)/shard_map/ppermute | solution.py:866
  139.0 20.9 %all-gather.8.cloned.1.call-done = bf16[1024,3072]{1,0:T(8,128)(2,1)} async-done(((bf16[32,3072]{1,0:T(8,128)(2,1)}), bf16[1024,3072]{1,0:T(8,128)(2,1)}) %all-gather.8.cloned.1.call-update) | async-done | bytes 6291472 | tf_op jit(solution)/shard_map/all_gather | solution.py:917
  159.9 4.7 %fusion.2 = f32[512,2048]{1,0:T(8,128)S(1)} fusion(bf16[1024,3072]{1,0:T(8,128)(2,1)} %all-gather.8.cloned.1.call-done, f32[512,1024]{1,0:T(8,128)S(1)} %get-tuple-element.147, f32[1024]{0:T(1024)S(1)} %bitcast.96, f32[512]{0:T(512)S(1)} %get-tuple-element.167), kind=kOutput, calls=%fused_computation.4 | convolution fusion | flops 2149056512 | bytes 10491904 | tf_op jit(solution)/shard_map/dot_general | solution.py:65
  164.6 3.5 fusion.6
  168.1 1.3 convert_bitcast_fusion
  169.5 2.5 convolution_convert_fusion
  172.0 3.2 pad_maximum_fusion
  175.3 5.2 %fusion.16 = bf16[512,1024]{1,0:T(8,128)(2,1)S(1)} fusion(bf16[1024,3072]{1,0:T(8,128)(2,1)} %all-gather.8.cloned.1.call-done, bf16[512,1024]{1,0:T(8,128)(2,1)} %copy-done.19, bf16[512,1024]{1,0:T(8,128)(2,1)} %copy-done.18), kind=kOutput, calls=%fused_computation.31 | convolution fusion | flops 2152202240 | bytes 7340032 | tf_op jit(solution)/shard_map/dot_general | solution.py:57
  180.5 3.1 collective-permute-start.3
  183.5 3.0 fusion.13
  186.5 20.9 %collective-permute-done.3 = bf16[512,1024]{1,0:T(8,128)(2,1)S(1)} collective-permute-done((bf16[512,1024]{1,0:T(8,128)(2,1)S(1)}, bf16[512,1024]{1,0:T(8,128)(2,1)S(1)}, u32[]{:S(2)}, u32[]{:S(2)}) %collective-permute-start.3) | collective-permute-done | bytes 1048608 | tf_op jit(solution)/shard_map/ppermute | solution.py:866
  207.8 3.3 collective-permute-start.4
  212.1 21.9 %collective-permute-done.4 = bf16[512,1024]{1,0:T(8,128)(2,1)S(1)} collective-permute-done((bf16[512,1024]{1,0:T(8,128)(2,1)S(1)}, bf16[512,1024]{1,0:T(8,128)(2,1)S(1)}, u32[]{:S(2)}, u32[]{:S(2)}) %collective-permute-start.4) | collective-permute-done | bytes 1048608 | tf_op jit(solution)/shard_map/ppermute | solution.py:866
  234.1 2.5 fusion.25
  236.6 1.3 fusion.28
  237.9 1.3 slice.134.dgated
  239.9 6.0 %shard_map.326 = (f32[512,768]{1,0:T(8,128)}, bf16[512,768]{1,0:T(8,128)(2,1)}, bf16[128,768]{1,0:T(8,128)(2,1)}) custom-call(f32[512,768]{1,0:T(8,128)} %slice.134.dgated, f32[512,768]{1,0:T(8,128)} %get-tuple-element.64.z, f32[512,768]{1,0:T(8,128)} %get-tuple-element.69.y, f32[512,1024]{1,0:T(8,128)} %get-tuple-element.60.pre, ...), custom_call_target="tpu_custom_call" | custom-call | tf_op jit(solution)/shard_map/pallas_call | solution.py:43
  245.9 1.3 collective-permute-start.5
  247.2 9.3 %shard_map.328 = (bf16[512,256]{1,0:T(8,128)(2,1)}, f32[512,128]{1,0:T(8,128)}, bf16[512,128]{1,0:T(8,128)(2,1)}) custom-call(bf16[512,256]{1,0:T(8,128)(2,1)} %get-tuple-element.52.q, bf16[512,128]{1,0:T(8,128)(2,1)} %get-tuple-element.53.k2, bf16[512,128]{1,0:T(8,128)(2,1)} %get-tuple-element.54.v2, bf16[512,128]{1,0:T(8,128)(2,1)} %get-tuple-element.55.k2p, ...), custom_call_target="tpu_custom_call" | custom-call | tf_op jit(solution)/shard_map/pallas_call | solution.py:43
  256.5 1.7 collective-permute-start.7
  259.6 13.2 %shard_map.327 = (f32[512,1024]{1,0:T(8,128)}, bf16[512,128]{1,0:T(8,128)(2,1)}, f32[8,128]{1,0:T(8,128)}) custom-call(f32[512,768]{1,0:T(8,128)} %get-tuple-element.70.dy, f32[512,1024]{1,0:T(8,128)} %get-tuple-element.60.pre, f32[512,128]{1,0:T(8,128)} %get-tuple-element.61.dt, f32[512,128]{1,0:T(8,128)} %get-tuple-element.62.cum, ...), custom_call_target="tpu_custom_call" | custom-call | tf_op jit(solution)/shard_map/pallas_call | solution.py:43
  273.5 1.3 collective-permute-start.6
  275.7 3.6 collective-permute-done.6.dpre_next
  279.9 8.0 %shard_map.329 = (bf16[512,2304]{1,0:T(8,128)(2,1)}, f32[8,1024]{1,0:T(8,128)}) custom-call(f32[512,1024]{1,0:T(8,128)} %get-tuple-element.73.dpre, f32[8,1024]{1,0:T(8,128)} %copy-done.10, f32[528,1024]{1,0:T(8,128)} %get-tuple-element.58.cin, f32[4,1024]{1,0:T(4,128)} %maximum_convert_fusion.taps, s32[528,1]{1,0:T(8,128)} %broadcast_in_dim.70.seg_ext, ...), custom_call_target="tpu_custom_call" | custom-call | tf_op jit(solution)/shard_map/pallas_call | solution.py:43
  287.9 1.4 pad_maximum_fusion.6.small
  289.3 59.4 %shard_map.330 = (f32[32,3328]{1,0:T(8,128)}, f32[512,1024]{1,0:T(8,128)}, f32[8,1152]{1,0:T(8,128)}) custom-call(bf16[512,1024]{1,0:T(8,128)(2,1)} %get-tuple-element.67.normed, bf16[512,2304]{1,0:T(8,128)(2,1)} %get-tuple-element.80.grads, bf16[512,1024]{1,0:T(8,128)(2,1)} %copy-done.1, bf16[512,1024]{1,0:T(8,128)(2,1)} %copy-done.3, ...), custom_call_target="tpu_custom_call" | custom-call | tf_op jit(solution)/shard_map/pallas_call | solution.py:820
  351.2 1.3 slice.118
  352.5 1.3 slice.119
  356.0 1.5 slice_reduce_fusion
  357.5 1.4 fusion.26
  358.9 1.5 slice_bitcast_fusion.1
  361.6 1.3 slice_bitcast_fusion.4
  363.0 3.4 collective-permute-done.8
  368.9 1.3 copy.102
  (107 shorter events, 33.6 us)
Async XLA Ops:
  7.2 55.2 %all-gather.4.cloned.1.call-start = ((), (), s32[]{:S(2)}) async-start(), calls=%async_computation.1 | async-start | bytes 4866048 | tf_op jit(solution)/shard_map/all_gather | solution.py:917
  12.7 95.7 %all-gather.6.cloned.1.call-start = ((), (), s32[]{:S(2)}) async-start(), calls=%async_computation.2 | async-start | bytes 2162688 | tf_op jit(solution)/shard_map/all_gather | solution.py:917
  14.3 145.6 %all-gather.8.cloned.1.call-start = ((), (), s32[]{:S(2)}) async-start(), calls=%async_computation.3 | async-start | bytes 6488064 | tf_op jit(solution)/shard_map/all_gather | solution.py:917
  16.8 343.7 %reduce-scatter.2.cloned.1.call-start = ((), (), s32[]{:S(2)}) async-start(), calls=%async_computation.4 | async-start | bytes 6488064 | tf_op jit(solution)/shard_map/reduce_scatter | solution.py:967
  16.9 47.4 %collective-permute-start = (bf16[512,1024]{1,0:T(8,128)(2,1)}, bf16[512,1024]{1,0:T(8,128)(2,1)S(1)}, u32[]{:S(2)}, u32[]{:S(2)}) collective-permute-start(bf16[512,1024]{1,0:T(8,128)(2,1)} %bitcast.74), channel_id=1, source_target_pairs={{0,2},{1,3},{4,6},{5,7},{8,10},{9,11},{12,14},{13,15},{16,18},{17,... | collective-permute-start | bytes 3145736 | tf_op jit(solution)/shard_map/ppermute | solution.py:899
  21.2 5.9 %copy-start.14 = (f32[12]{0:T(128)S(1)}, f32[12]{0:T(128)}, u32[]{:S(2)}) copy-start(f32[12]{0:T(128)} %param.34) | copy-start | bytes 148
  21.2 6.6 %copy-start.17 = (f32[12]{0:T(128)S(1)}, f32[12]{0:T(128)}, u32[]{:S(2)}) copy-start(f32[12]{0:T(128)} %param.32) | copy-start | bytes 148
  21.2 6.6 %copy-start.15 = (f32[12]{0:T(128)S(1)}, f32[12]{0:T(128)}, u32[]{:S(2)}) copy-start(f32[12]{0:T(128)} %param.33) | copy-start | bytes 148
  21.2 7.2 %copy-start.11 = (bf16[4,768]{1,0:T(4,128)(2,1)S(1)}, bf16[4,768]{1,0:T(4,128)(2,1)}, u32[]{:S(2)}) copy-start(bf16[4,768]{1,0:T(4,128)(2,1)} %param.30) | copy-start | bytes 18436
  21.2 7.1 %copy-start.13 = (bf16[4,256]{1,0:T(4,128)(2,1)S(1)}, bf16[4,256]{1,0:T(4,128)(2,1)}, u32[]{:S(2)}) copy-start(bf16[4,256]{1,0:T(4,128)(2,1)} %param.31) | copy-start | bytes 6148
  64.3 1.0 copy-start.4
  82.0 11.4 %collective-permute-start.1 = (bf16[128,768]{1,0:T(8,128)(2,1)}, bf16[128,768]{1,0:T(8,128)(2,1)S(1)}, u32[]{:S(2)}, u32[]{:S(2)}) collective-permute-start(bf16[128,768]{1,0:T(8,128)(2,1)} %get-tuple-element.63), channel_id=1, source_target_pairs={{0,2},{1,3},{4,6},{5,7},{8,10},{9,11},{12,14},{13,15},{16,18},{17,... | collective-permute-start | bytes 589832 | tf_op jit(solution)/shard_map/ppermute | solution.py:940
  93.4 0.7 copy-start.8
  102.6 8.7 %copy-start.3 = (bf16[512,1024]{1,0:T(8,128)(2,1)}, bf16[512,1024]{1,0:T(8,128)(2,1)S(1)}, u32[]{:S(2)}) copy-start(bf16[512,1024]{1,0:T(8,128)(2,1)S(1)} %constant_dynamic-update-slice_fusion.mixed) | copy-start | bytes 3145732
  102.6 35.8 %copy-start = (bf16[1,512,1024]{2,1,0:T(8,128)(2,1)S(1)}, bf16[1,512,1024]{2,1,0:T(8,128)(2,1)}, u32[]{:S(2)}) copy-start(bf16[1,512,1024]{2,1,0:T(8,128)(2,1)} %param.19) | copy-start | bytes 3145732
  111.4 27.1 %collective-permute-start.2 = (bf16[512,1024]{1,0:T(8,128)(2,1)S(1)}, bf16[512,1024]{1,0:T(8,128)(2,1)S(1)}, u32[]{:S(2)}, u32[]{:S(2)}) collective-permute-start(bf16[512,1024]{1,0:T(8,128)(2,1)S(1)} %convolution_convert_fusion.1), channel_id=1, source_target_pairs={{0,1},{1,0},{2,3},{3,2},{4,5},{5,4},{6,7},{7,6},{8,9},{9,8},{10,11... | collective-permute-start | bytes 3145736 | tf_op jit(solution)/shard_map/ppermute | solution.py:866
  159.9 4.7 %copy-start.5 = (bf16[1,512,1024]{2,1,0:T(8,128)(2,1)S(1)}, bf16[1,512,1024]{2,1,0:T(8,128)(2,1)}, u32[]{:S(2)}) copy-start(bf16[1,512,1024]{2,1,0:T(8,128)(2,1)} %param.21) | copy-start | bytes 3145732
  168.1 1.3 copy-start.18
  168.1 1.3 copy-start.19
  180.5 26.9 %collective-permute-start.3 = (bf16[512,1024]{1,0:T(8,128)(2,1)S(1)}, bf16[512,1024]{1,0:T(8,128)(2,1)S(1)}, u32[]{:S(2)}, u32[]{:S(2)}) collective-permute-start(bf16[512,1024]{1,0:T(8,128)(2,1)S(1)} %fusion.16), channel_id=1, source_target_pairs={{0,1},{1,0},{2,3},{3,2},{4,5},{5,4},{6,7},{7,6},{8,9},{9,8},{10,11... | collective-permute-start | bytes 3145736 | tf_op jit(solution)/shard_map/ppermute | solution.py:866
  207.7 26.3 %copy-start.6 = (bf16[1,512,1024]{2,1,0:T(8,128)(2,1)S(1)}, bf16[1,512,1024]{2,1,0:T(8,128)(2,1)}, u32[]{:S(2)}) copy-start(bf16[1,512,1024]{2,1,0:T(8,128)(2,1)} %param.21) | copy-start | bytes 3145732
  207.8 26.3 %collective-permute-start.4 = (bf16[512,1024]{1,0:T(8,128)(2,1)S(1)}, bf16[512,1024]{1,0:T(8,128)(2,1)S(1)}, u32[]{:S(2)}, u32[]{:S(2)}) collective-permute-start(bf16[512,1024]{1,0:T(8,128)(2,1)S(1)} %fusion.13), channel_id=1, source_target_pairs={{0,1},{1,0},{2,3},{3,2},{4,5},{5,4},{6,7},{7,6},{8,9},{9,8},{10,11... | collective-permute-start | bytes 3145736 | tf_op jit(solution)/shard_map/ppermute | solution.py:866
  234.1 2.5 copy-start.16
  236.6 1.3 copy-start.1
  245.9 13.0 %collective-permute-start.5 = (bf16[128,768]{1,0:T(8,128)(2,1)}, bf16[128,768]{1,0:T(8,128)(2,1)S(1)}, u32[]{:S(2)}, u32[]{:S(2)}) collective-permute-start(bf16[128,768]{1,0:T(8,128)(2,1)} %get-tuple-element.72), channel_id=1, source_target_pairs={{2,0},{3,1},{6,4},{7,5},{10,8},{11,9},{14,12},{15,13},{18,16},{19,... | collective-permute-start | bytes 589832 | tf_op jit(solution)/shard_map/ppermute | solution.py:972
  256.5 19.2 %collective-permute-start.7 = (bf16[512,128]{1,0:T(8,128)(2,1)}, bf16[512,128]{1,0:T(8,128)(2,1)S(1)}, u32[]{:S(2)}, u32[]{:S(2)}) collective-permute-start(bf16[512,128]{1,0:T(8,128)(2,1)} %get-tuple-element.76), channel_id=1, source_target_pairs={{2,0},{3,1},{6,4},{7,5},{10,8},{11,9},{14,12},{15,13},{18,16},{19,... | collective-permute-start | bytes 393224 | tf_op jit(solution)/shard_map/ppermute | solution.py:976
  258.9 0.7 copy-start.7
  273.5 5.8 %collective-permute-start.6 = (f32[8,1024]{1,0:T(8,128)S(1)}, f32[8,1024]{1,0:T(8,128)S(1)}, u32[]{:S(2)}, u32[]{:S(2)}) collective-permute-start(f32[8,1024]{1,0:T(8,128)S(1)} %slice.107), channel_id=1, source_target_pairs={{2,0},{3,1},{6,4},{7,5},{10,8},{11,9},{14,12},{15,13},{18,16},{19,... | collective-permute-start | bytes 98312 | tf_op jit(solution)/shard_map/ppermute | solution.py:980
  275.7 3.7 copy-start.9
  279.3 0.6 copy-start.10
  279.9 8.0 %copy-start.12 = (f32[8,128]{1,0:T(8,128)S(1)}, f32[8,128]{1,0:T(8,128)}, u32[]{:S(2)}) copy-start(f32[8,128]{1,0:T(8,128)} %get-tuple-element.82) | copy-start | bytes 12292
  348.6 20.3 %copy-start.2 = (f32[512,1024]{1,0:T(8,128)S(1)}, f32[512,1024]{1,0:T(8,128)}, u32[]{:S(2)}) copy-start(f32[512,1024]{1,0:T(8,128)} %get-tuple-element.83) | copy-start | bytes 6291460
  360.5 5.9 %collective-permute-start.8 = (bf16[32,3072]{1,0:T(8,128)(2,1)}, bf16[32,3072]{1,0:T(8,128)(2,1)S(1)}, u32[]{:S(2)}, u32[]{:S(2)}) collective-permute-start(bf16[32,3072]{1,0:T(8,128)(2,1)} %reduce-scatter.2.cloned.1.call-done), channel_id=1, source_target_pairs={{0,2},{2,0},{1,3},{3,1},{4,6},{6,4},{5,7},{7,5},{8,10},{10,8},{9,1... | collective-permute-start | bytes 589832 | tf_op jit(solution)/shard_map/ppermute | solution.py:866
Sparse Core Ops, SparseCore 0:
  12.9 49.4 all-gather.3
  65.2 43.2 all-gather.5
  111.3 48.5 all-gather.7
  175.4 85.2 reduce-scatter.1
